TPU v7x, 256 devices: a whole 4x4x8 slice. The times are simulated.
256 devices in a mesh: orient: 64 (over x_lo, y, z), zslab: 4 (over x_hi, core).
Axes of the slice: x: 4 (x_hi: 2, x_lo: 2; x = x_hi * 2 + x_lo), y: 4, z: 8, core: 2. Of those that a mesh axis runs over, the one named last changes fastest.
Arguments:
- volume: float32 [32, 256, 256], P('zslab'), may hold values from -60 to 60, as said below
- templates: float32 [64, 16, 16, 16], P('orient'), may hold values from -6 to 6
- wedge: int32 [16, 16, 16], replicated, may hold values 0 or 1
Outputs:
- best: float32 [32, 256, 256], P('zslab', 'orient')
Inputs may be any that keep to these rules, and one draw needn't show every extreme that they name: `volume`: A tomogram whose contrast varies between z layers and between x planes.
All inputs are finite; a program needn't handle non-finite values.
Results may differ from a plain program's by a relative error of at most 0.0001.
Values sent between devices are 32-bit elements; how exact they have to be, the bound alone decides.
No kernel may reach another device: no remote copies, remote signals or barrier semaphores. Data moves between devices by JAX's collectives and lax.ppermute only.
A program may use at most 128 MiB of HBM per device.

v0:
```python
import math

import jax
import jax.numpy as jnp
from jax import lax
from jax.sharding import PartitionSpec as P

TS = 16


forms = ("kj,jab->kab", "kj,ajb->akb", "kj,abj->abk")


def padded_2(cells, sides, width):
    for axis, dim in sides:
        count = lax.axis_size(axis)
        ends = count - 1
        head = lax.slice_in_dim(cells, 0, width, axis=dim)
        tail = lax.slice_in_dim(cells, cells.shape[dim] - width, cells.shape[dim], axis=dim)
        cells = jnp.concatenate(
            [
                lax.ppermute(tail, axis, [(i, (i + 1) % count) for i in range(ends)]),
                cells,
                lax.ppermute(head, axis, [((i + 1) % count, i) for i in range(ends)]),
            ],
            axis=dim,
        )
    return cells


def table(rows, cols, count):
    phase = rows[:, None] * (cols[None, :] % count) % count
    angle = phase.astype(jnp.float32) * (2.0 * math.pi / count)
    return (jnp.cos(angle), jnp.sin(angle))


def matmul_axis(matrix, field, axis):
    return jnp.einsum(forms[axis], matrix, field, precision=lax.Precision.HIGHEST)


def along(real_part, imag_part, tables, sign, axis):
    cosine, sine = tables
    if imag_part is None:
        return (matmul_axis(cosine, real_part, axis), sign * matmul_axis(sine, real_part, axis))
    out_real = matmul_axis(cosine, real_part, axis) - sign * matmul_axis(sine, imag_part, axis)
    out_imag = matmul_axis(cosine, imag_part, axis) + sign * matmul_axis(sine, real_part, axis)
    return (out_real, out_imag)


def real_along(real_part, imag_part, tables, sign, axis):
    cosine, sine = tables
    return matmul_axis(cosine, real_part, axis) - sign * matmul_axis(sine, imag_part, axis)


def window_sum(field, count, axis):
    doubled = field
    summed_rows = None
    offset = 0
    stride = 1
    for bit_number in range(count.bit_length()):
        if count >> bit_number & 1:
            shifted = jnp.roll(doubled, -offset, axis=axis)
            summed_rows = shifted
            offset = offset + stride
        if bit_number + 1 < count.bit_length():
            doubled = doubled + jnp.roll(doubled, -stride, axis=axis)
            stride = stride * 2
    return jnp.roll(summed_rows, count // 2, axis=axis)


def shards(volume, templates, wedge):
    half = TS // 2
    slab = volume.shape[0]
    rows_x = volume.shape[1]
    rows_y = volume.shape[2]
    small = table(jnp.arange(TS), jnp.arange(TS), TS)
    template = templates[0]
    spec_real, spec_imag = along(template, None, small, -1.0, 0)
    spec_real, spec_imag = along(spec_real, spec_imag, small, -1.0, 1)
    spec_real, spec_imag = along(spec_real, spec_imag, small, -1.0, 2)
    keep = wedge.astype(jnp.float32)
    spec_real, spec_imag = (spec_real * keep, spec_imag * keep)
    spec_real, spec_imag = along(spec_real, spec_imag, small, 1.0, 0)
    spec_real, spec_imag = along(spec_real, spec_imag, small, 1.0, 1)
    filt = real_along(spec_real, spec_imag, small, 1.0, 2) / float(TS**3)
    centered = filt - jnp.mean(filt)
    normed = centered / jnp.sqrt(jnp.sum(centered * centered) + 1e-05)
    padded = padded_2(volume, (("zslab", 0),), half)
    length = padded.shape[0]
    offsets = jnp.arange(TS) - half
    tmpl_real, tmpl_imag = along(normed, None, table(jnp.arange(length), offsets, length), -1.0, 0)
    tmpl_real, tmpl_imag = along(
        tmpl_real, tmpl_imag, table(jnp.arange(rows_x), offsets, rows_x), -1.0, 1
    )
    tmpl_real, tmpl_imag = along(
        tmpl_real, tmpl_imag, table(jnp.arange(rows_y), offsets, rows_y), -1.0, 2
    )
    tmpl_imag = -tmpl_imag
    table_y = table(jnp.arange(rows_y), jnp.arange(rows_y), rows_y)
    table_z = table(jnp.arange(length), jnp.arange(length), length)
    block = rows_x // lax.axis_size("orient")
    first_row = lax.axis_index("orient") * block
    rows = first_row + jnp.arange(block)
    vol_real, vol_imag = along(padded, None, table(rows, jnp.arange(rows_x), rows_x), -1.0, 1)
    vol_real, vol_imag = along(vol_real, vol_imag, table_y, -1.0, 2)
    vol_real, vol_imag = along(vol_real, vol_imag, table_z, -1.0, 0)
    vol_real, vol_imag = (
        lax.all_gather(vol_real, "orient", axis=1, tiled=True),
        lax.all_gather(vol_imag, "orient", axis=1, tiled=True),
    )
    prod_real = tmpl_real * vol_real - tmpl_imag * vol_imag
    prod_imag = tmpl_real * vol_imag + tmpl_imag * vol_real
    inner = table(half + jnp.arange(slab), jnp.arange(length), length)
    prod_real, prod_imag = along(prod_real, prod_imag, inner, 1.0, 0)
    prod_real, prod_imag = along(prod_real, prod_imag, table_y, 1.0, 2)
    corr = real_along(
        prod_real, prod_imag, table(jnp.arange(rows_x), jnp.arange(rows_x), rows_x), 1.0, 1
    )
    corr = corr / float(length * rows_x * rows_y)
    squared = padded * padded
    layers = jnp.arange(slab)[:, None]
    window_z = (
        (jnp.arange(length)[None, :] - layers >= 0) & (jnp.arange(length)[None, :] - layers < TS)
    ).astype(jnp.float32)
    energy = matmul_axis(window_z, squared, 0)
    energy = window_sum(energy, TS, 1)
    energy = window_sum(energy, TS, 2)
    score = corr / jnp.sqrt(energy / float(TS**3) + 1e-05)
    groups = lax.axis_size("orient")
    block = rows_x // groups
    whole = lax.pmax(score, "orient")
    return lax.dynamic_slice_in_dim(whole, lax.axis_index("orient") * block, block, 1)


def solution(mesh):
    return jax.shard_map(
        shards,
        mesh=mesh,
        in_specs=(P("zslab", None, None), P("orient", None, None, None), P()),
        out_specs=P("zslab", "orient", None),
        check_vma=False,
    )
```

profile of v0, /device:TPU:4, one launch (start us, length us, event | category | flops | bytes accessed | tf_op | source)
XLA Modules:
  0.0 1361.5 jit_solution(7359783156009963004)
XLA Ops:
  6.5 2.0 collective-permute-start
  8.6 5.1 collective-permute-start.1
  13.8 22.0 %collective-permute-done = f32[8,256,256]{2,1,0:T(8,128)} collective-permute-done((f32[8,256,256]{2,1,0:T(8,128)}, f32[8,256,256]{2,1,0:T(8,128)}, u32[]{:S(2)}, u32[]{:S(2)}) %collective-permute-start) | collective-permute-done | bytes 2097184 | tf_op jit(solution)/shard_map/ppermute | solution.py:22
  35.8 1.7 constant_dynamic-update-slice_fusion.2
  38.0 3.4 fusion.46
  41.4 3.4 convolution_bitcast_fusion
  44.8 1.3 fusion.60
  46.1 1.3 fusion.62
  47.4 1.3 fusion.47
  49.0 10.7 fusion.48
  68.4 1.0 fusion.144
  69.5 1.0 fusion.38
  78.5 5.5 fusion.105
  84.0 7.2 fusion.102
  91.3 7.7 multiply_subtract_fusion.1
  100.1 7.0 fusion
  107.1 2.1 copy.86
  117.0 254.6 %all-gather.5.cloned.1.call-done = f32[24,256,256]{2,0,1:T(8,128)} async-done(((f32[24,4,256]{2,0,1:T(8,128)}), f32[24,256,256]{2,0,1:T(8,128)}) %all-gather.5.cloned.1.call-update) | async-done | bytes 6291472 | tf_op jit(solution)/shard_map/all_gather | solution.py:109
  371.5 307.4 %all-gather.3.cloned.1.call-done = f32[24,256,256]{2,0,1:T(8,128)} async-done(((f32[24,4,256]{2,0,1:T(8,128)}), f32[24,256,256]{2,0,1:T(8,128)}) %all-gather.3.cloned.1.call-update) | async-done | bytes 6291472 | tf_op jit(solution)/shard_map/all_gather | solution.py:108
  678.9 16.0 %multiply_subtract_fusion = (f32[24,256,256]{2,1,0:T(8,128)S(1)}, f32[24,256,256]{2,1,0:T(8,128)S(1)}) fusion(f32[24,256,256]{2,1,0:T(8,128)} %multiply_subtract_fusion.1, f32[24,256,256]{2,0,1:T(8,128)} %all-gather.5.cloned.1.call-done, f32[24,256,256]{2,0,1:T(8,128)} %all-gather.3.cloned.1.call-done, f32[24,256,256]{2,1,0:T(8,128)} %fusion.102, ...), kind=kOutput, calls=%fused_computation.3 | convolution fusion | flops 316203008 | bytes 38142016 | tf_op jit(solution)/shard_map/kj,abj->abk/dot_general | solution.py:38
  694.9 6.8 fusion.2
  701.8 7.1 fusion.4
  708.9 6.9 fusion.27
  715.9 3.8 fusion.23
  719.7 3.4 fusion.25
  723.1 7.0 fusion.30
  730.1 3.6 fusion.19
  733.7 3.4 fusion.21
  737.2 2.9 fusion.15
  740.1 4.4 fusion.14
  744.5 607.8 %all-reduce.2.cloned.1.call-done = f32[8,256,256]{1,2,0:T(8,128)} async-done(((f32[8,256,256]{1,2,0:T(8,128)}), f32[8,256,256]{1,2,0:T(8,128)}) %all-reduce.2.cloned.1.call-update) | async-done | bytes 2097168 | tf_op jit(solution)/shard_map/pmax | solution.py:131
  1352.3 1.6 constant_dynamic-slice_fusion
  (100 shorter events, 25.3 us)
Async XLA Ops:
  6.5 55.5 %copy-start = (f32[1,16,16,16]{3,2,1,0:T(8,128)S(1)}, f32[1,16,16,16]{3,2,1,0:T(8,128)}, u32[]{:S(2)}) copy-start(f32[1,16,16,16]{3,2,1,0:T(8,128)} %param.4) | copy-start | bytes 49156
  6.5 365.0 %all-gather.5.cloned.1.call-start = ((), (), s32[]{:S(2)}) async-start(), calls=%async_computation.1 | async-start | bytes 6389760 | tf_op jit(solution)/shard_map/all_gather | solution.py:109
  6.5 29.3 %collective-permute-start = (f32[8,256,256]{2,1,0:T(8,128)}, f32[8,256,256]{2,1,0:T(8,128)}, u32[]{:S(2)}, u32[]{:S(2)}) collective-permute-start(f32[8,256,256]{2,1,0:T(8,128)} %param.3), channel_id=1, source_target_pairs={{0,1},{1,2},{2,3},{4,5},{5,6},{6,7},{8,9},{9,10},{10,11},{12,13},{... | collective-permute-start | bytes 6291464 | tf_op jit(solution)/shard_map/ppermute | solution.py:22
  8.6 29.2 %collective-permute-start.1 = (f32[8,256,256]{2,1,0:T(8,128)}, f32[8,256,256]{2,1,0:T(8,128)S(1)}, u32[]{:S(2)}, u32[]{:S(2)}) collective-permute-start(f32[8,256,256]{2,1,0:T(8,128)} %param.3), channel_id=1, source_target_pairs={{1,0},{2,1},{3,2},{5,4},{6,5},{7,6},{9,8},{10,9},{11,10},{13,12},{... | collective-permute-start | bytes 6291464 | tf_op jit(solution)/shard_map/ppermute | solution.py:24
  13.8 23.8 %copy-start.4 = (f32[8,256,256]{2,1,0:T(8,128)S(1)}, f32[8,256,256]{2,1,0:T(8,128)}, u32[]{:S(2)}) copy-start(f32[8,256,256]{2,1,0:T(8,128)} %param.3) | copy-start | bytes 6291460
  38.0 3.4 copy-start.2
  59.7 5.3 copy-start.5
  60.7 618.2 %all-gather.3.cloned.1.call-start = ((), (), s32[]{:S(2)}) async-start(), calls=%async_computation | async-start | bytes 6389760 | tf_op jit(solution)/shard_map/all_gather | solution.py:108
  62.0 1290.3 %all-reduce.2.cloned.1.call-start = ((), (), s32[]{:S(2)}) async-start(), calls=%async_computation.2 | async-start | bytes 4194304 | tf_op jit(solution)/shard_map/pmax | solution.py:131
  84.0 15.0 %slice-start = ((s8[6291456]{0:T(1024)(128)(4,1)}), s8[4194304]{0:T(1024)(128)(4,1)S(1)}, s32[]{:S(2)}) async-start(s8[6291456]{0:T(1024)(128)(4,1)} %bitcast.169), calls=%async_computation.3 | async-start | bytes 8388608
  91.3 7.7 slice-start.1
  116.9 578.0 %copy-start.3 = (f32[8,256,256]{1,2,0:T(8,128)}, f32[8,256,256]{1,2,0:T(8,128)S(1)}, u32[]{:S(2)}) copy-start(f32[8,256,256]{1,2,0:T(8,128)S(1)} %maximum_add_fusion.6) | copy-start | bytes 6291460
  737.1 2.9 slice-start.2
  737.1 2.9 slice-start.3
  744.5 610.4 %copy-start.1 = (f32[1,16,16,16]{3,2,1,0:T(8,128)S(1)}, f32[1,16,16,16]{3,2,1,0:T(8,128)}, u32[]{:S(2)}) copy-start(f32[1,16,16,16]{3,2,1,0:T(8,128)} %param.4) | copy-start | bytes 49156
Sparse Core Ops, SparseCore 0:
  60.8 310.6 all-gather.4
  373.3 305.5 all-gather.2
  744.6 607.6 all-reduce.1
where the time goes:
time: 1370 us; the launch traced here: 1360 us
  waiting for transfers between devices  1190 us (87%)
  matrix products  130 us (9%)
  between operations  15.3 us (1%)
    pmax x1, waiting for transfers between devices, shards(): whole = lax.pmax(score, 'orient')  608 us
    all_gather x1, waiting for transfers between devices, shards(): lax.all_gather(vol_real, 'orient', axis=1, tiled=True)  307 us
    all_gather x1, waiting for transfers between devices, shards(): lax.all_gather(vol_imag, 'orient', axis=1, tiled=True)  255 us
    dot_general x49, matrix products, matmul_axis(): jnp.einsum(forms[axis], matrix, field, precision=lax.Precision.HIGHEST)  129 us
  transfers between devices with their start and end apart: 5, of which 4 were waited for; matrix products, arithmetic and copies ran while one was open for 4% of the time, Pallas kernels for 0%

commit v1 on v0

v1 whole, which is shorter than its diff:
```python
import math

import jax
import jax.numpy as jnp
import numpy as np
from jax import lax
from jax.experimental import pallas as pl
from jax.experimental.pallas import tpu as pltpu
from jax.sharding import PartitionSpec as P

TS = 16
HALF = 8
NF = 32
NK = 16
SLAB = 8
NY = 256
GROUP = 4
NO = 16
STRIP = 4
LANES = 128
KDIM = TS * 48
EXACT = lax.Precision.HIGHEST
VMEM = pl.BlockSpec(memory_space=pltpu.VMEM)
SMEM = pl.BlockSpec(memory_space=pltpu.SMEM)


def plus(a, b):
    if a is None:
        return b
    return a if b is None else a + b


def minus(a, b):
    if b is None:
        return a
    return -b if a is None else a - b


def twiddled(value, k, count, sign):
    re, im = value
    if k == 0:
        return value
    if 4 * k == count:
        return (None if im is None else -sign * im, None if re is None else sign * re)
    c = math.cos(2.0 * math.pi * k / count)
    s = sign * math.sin(2.0 * math.pi * k / count)
    if im is None:
        return (c * re, s * re)
    if re is None:
        return (-s * im, c * im)
    return (c * re - s * im, s * re + c * im)


def forward(rows):
    count = len(rows)
    if count == 2:
        return [(plus(rows[0], rows[1]), None), (minus(rows[0], rows[1]), None)]
    even, odd = forward(rows[::2]), forward(rows[1::2])
    bins = [None] * (count // 2 + 1)
    for k in range(count // 4 + 1):
        e, o = even[k], twiddled(odd[k], k, count, -1.0)
        bins[k] = (plus(e[0], o[0]), plus(e[1], o[1]))
        if 4 * k != count:
            re, im = minus(e[0], o[0]), minus(e[1], o[1])
            bins[count // 2 - k] = (re, None if im is None else -im)
    return bins


def inverse(bins, count, need):
    if count == 2:
        first = bins[0][0] + bins[1][0]
        return [first] if need == 1 else [first, bins[0][0] - bins[1][0]]
    even, odd = [], []
    for k in range(count // 4 + 1):
        a, b = bins[k], bins[count // 2 - k]
        if k == 0:
            even.append((a[0] + b[0], None))
            odd.append((a[0] - b[0], None))
        elif 4 * k == count:
            even.append((2.0 * a[0], None))
            odd.append((-2.0 * a[1], None))
        else:
            even.append((a[0] + b[0], a[1] - b[1]))
            odd.append(twiddled((a[0] - b[0], a[1] + b[1]), k, count, 1.0))
    evens = inverse(even, count // 2, (need + 1) // 2)
    odds = inverse(odd, count // 2, need // 2)
    rows = [None] * need
    rows[::2] = evens
    rows[1::2] = odds
    return rows


def slots(bins):
    return [(bins[0][0], bins[NK][0])] + [bins[k] for k in range(1, NK)]


def unslot(pairs):
    return [(pairs[0][0], None)] + list(pairs[1:]) + [(pairs[0][1], None)]


def halves(value):
    high = value.astype(jnp.bfloat16)
    return high, (value - high.astype(jnp.float32)).astype(jnp.bfloat16)


def filter_tables():
    small = np.arange(TS)
    pair = 2.0 * math.pi * np.outer(small, small) / TS
    two = pair[:, None, :, None] + pair[None, :, None, :]
    two = two.reshape(TS * TS, TS * TS)
    right = np.concatenate([np.cos(two), -np.sin(two)], axis=1)
    c, s = np.cos(pair), np.sin(pair)
    ahead = np.block([[c, s], [-s, c]])
    back = np.block([[c, -s], [s, c]])
    return tuple(np.asarray(t, np.float32) for t in (right, ahead, back))


def spread_table():
    out = np.zeros((TS, TS, TS, 48), np.float32)
    for b in range(TS):
        for c in range(TS):
            out[b, c, b, c] = 1.0
    return out.reshape(TS * TS, KDIM)


def filter_kernel(template_ref, wedge_ref, right_ref, ahead_ref, back_ref, out_ref):
    def product(a, b):
        return jnp.dot(a, b, precision=EXACT, preferred_element_type=jnp.float32)

    width = TS * TS
    spec = product(template_ref[...], right_ref[...])
    spec = jnp.concatenate([spec[:, :width], spec[:, width:]], axis=0)
    keep = wedge_ref[...]
    spec = product(ahead_ref[...], spec) * jnp.concatenate([keep, keep], axis=0)
    spec = product(back_ref[...], spec)
    filt = product(spec[:TS], right_ref[:, :width]) + product(spec[TS:], right_ref[:, width:])
    filt = filt * (1.0 / float(TS**3))
    centered = filt - jnp.sum(filt) * (1.0 / float(TS**3))
    out_ref[...] = centered / jnp.sqrt(jnp.sum(centered * centered) + 1e-05)


def volume_kernel(place_ref, lower_ref, own_ref, upper_ref, high_ref, low_ref, scale_ref, spec_ref):
    for block, ref in enumerate((lower_ref, own_ref, upper_ref)):
        for lane in range(0, NY, LANES):
            bins = forward([ref[x, :, lane : lane + LANES] for x in range(NF)])
            for k, (re, im) in enumerate(slots(bins)):
                spec_ref[k, 8 * block : 8 * block + 8, lane : lane + LANES] = re
                spec_ref[k, 24 + 8 * block : 32 + 8 * block, lane : lane + LANES] = im

    def split(k, carry):
        high_ref[k], low_ref[k] = halves(spec_ref[k])
        return carry

    lax.fori_loop(0, NK, split, 0)
    first = place_ref[0] * STRIP
    sums = []
    for x in range(STRIP + TS - 1):
        layers = jnp.concatenate([r[first + x] for r in (lower_ref, own_ref, upper_ref)], axis=0)
        sums.append(layers * layers)
    for step in (1, 2, 4, 8):
        sums = [sums[i] + sums[i + step] for i in range(len(sums) - step)]
    for x in range(STRIP):
        total = sums[x]
        for step in (1, 2, 4, 8):
            total = total + pltpu.roll(total, 24 - step, axis=0)
        total = total[:SLAB]
        for step in (1, 2, 4, 8):
            total = total + pltpu.roll(total, NY - step, axis=1)
        total = pltpu.roll(total, HALF, axis=1)
        scale_ref[x] = (1.0 / NF) / jnp.sqrt(total * (1.0 / float(TS**3)) + 1e-05)


def score_kernel(
    place_ref, a_ref, b_ref, c_ref, d_ref, spread_ref, high_ref, low_ref,
    out0_ref, out1_ref, out2_ref, out3_ref,
    wide_ref, base_ref, base_high, base_low, left_ref, right_high, right_low, prod_ref, best_ref,
):
    for quarter, ref in enumerate((a_ref, b_ref, c_ref, d_ref)):
        high, low = halves(ref[...])
        rows = ref.shape[0]
        wide = jnp.dot(
            high, spread_ref[...], preferred_element_type=jnp.float32
        ) + jnp.dot(low, spread_ref[...], preferred_element_type=jnp.float32)
        for j in range(KDIM // LANES):
            wide_ref[j, rows * quarter : rows * quarter + rows, :] = wide[:, j * LANES : (j + 1) * LANES]
    for o in range(0, NO, 8):
        for lane in range(0, KDIM, LANES):
            rows = [
                wide_ref[lane // LANES, pl.ds(o * TS + a, 8, stride=TS), :] for a in range(TS)
            ]
            bins = forward(rows + [None] * (NF - TS))
            for k, (re, im) in enumerate(slots(bins)):
                base_ref[k, 0, o : o + 8, lane : lane + LANES] = re
                base_ref[k, 1, o : o + 8, lane : lane + LANES] = im

    def assemble(k, carry):
        re, im = base_ref[k, 0], base_ref[k, 1]
        packed = (k == 0).astype(jnp.float32)
        mixed = 1.0 - packed
        first = re + mixed * pltpu.roll(im, 24, axis=1)
        second = pltpu.roll(mixed * re + packed * im, 24, axis=1) - mixed * im
        base_high[k, 0], base_low[k, 0] = halves(first)
        base_high[k, 1], base_low[k, 1] = halves(second)
        return carry

    lax.fori_loop(0, NK, assemble, 0)

    def one(k, carry):
        for part in range(2):
            for row0, ref in ((0, base_high), (256, base_low)):
                value = ref[k, part]
                for z in range(SLAB):
                    at = row0 + part * 128 + z * NO
                    left_ref[at : at + NO, :] = value if z == 0 else pltpu.roll(value, z, axis=1)
        for src, dst in ((high_ref, right_high), (low_ref, right_low)):
            value = src[k]
            for b in range(TS):
                shift = (HALF - b) % NY
                dst[48 * b : 48 * b + 48, :] = value if shift == 0 else pltpu.roll(value, shift, axis=1)
        both = jnp.dot(left_ref[...], right_high[...], preferred_element_type=jnp.float32)
        low = jnp.dot(left_ref[:256], right_low[...], preferred_element_type=jnp.float32)
        prod_ref[k] = both[:256] + (both[256:] + low)
        return carry

    lax.fori_loop(0, NK, one, 0)

    best_ref[...] = jnp.zeros_like(best_ref)

    def finish(z, carry):
        row = pl.multiple_of(z * NO, NO)
        here = lax.broadcasted_iota(jnp.int32, (SLAB, LANES), 0) == z
        for lane in range(0, NY, LANES):
            top = None
            for o in (0, 8):
                pairs = [
                    (
                        prod_ref[k, pl.ds(row + o, 8), lane : lane + LANES],
                        prod_ref[k, pl.ds(128 + row + o, 8), lane : lane + LANES],
                    )
                    for k in range(NK)
                ]
                rows = inverse(unslot(pairs), NF, NF // 2)
                top = rows if top is None else [jnp.maximum(a, b) for a, b in zip(top, rows)]
            for x in range(NF // 2):
                largest = jnp.max(top[x], axis=0, keepdims=True)
                best_ref[x, :, lane : lane + LANES] = jnp.where(
                    here, largest, best_ref[x, :, lane : lane + LANES]
                )
        return carry

    lax.fori_loop(0, SLAB, finish, 0)
    mine = place_ref[0]
    for m, ref in enumerate((out0_ref, out1_ref, out2_ref, out3_ref)):
        ref[...] = best_ref[pl.ds((mine ^ m) * STRIP, STRIP)]


def last_kernel(scale_ref, a_ref, b_ref, c_ref, d_ref, out_ref):
    for x in range(STRIP):
        top = jnp.maximum(jnp.maximum(a_ref[x], b_ref[x]), jnp.maximum(c_ref[x], d_ref[x]))
        out_ref[:, x, :] = top * scale_ref[x]


def call(kernel, outs, scratch, args, specs, flops=0, nbytes=0):
    return pl.pallas_call(
        kernel,
        out_shape=outs,
        in_specs=specs,
        out_specs=[VMEM] * len(outs) if isinstance(outs, (list, tuple)) else VMEM,
        scratch_shapes=scratch,
        compiler_params=pltpu.CompilerParams(vmem_limit_bytes=48 * 1024 * 1024),
        cost_estimate=pl.CostEstimate(flops=flops, bytes_accessed=nbytes, transcendentals=0),
    )(*args)


def shards(volume, templates, wedge):
    f32, bf16 = jnp.float32, jnp.bfloat16
    count = lax.axis_size("orient")
    me = lax.axis_index("orient")
    place = (me % GROUP).astype(jnp.int32).reshape(1)
    region = me // GROUP

    def swap(value, mask):
        return lax.ppermute(value, "orient", [(i, i ^ mask) for i in range(count)])

    template = jnp.transpose(templates[0], (1, 2, 0)).reshape(TS, TS * TS)
    keep = jnp.transpose(wedge.astype(f32), (1, 2, 0)).reshape(TS, TS * TS)
    normed = call(
        filter_kernel, jax.ShapeDtypeStruct((TS, TS * TS), f32), [],
        (template, keep) + filter_tables(), [VMEM] * 5, 1 << 22, 1 << 20,
    )
    four = jnp.concatenate([normed] + [swap(normed, m) for m in (4, 16, 20)], axis=0)
    gathered = [four] + [swap(four, m) for m in (8, 32, 40)]

    rows = volume.shape[1]
    pieces = [
        lax.dynamic_slice_in_dim(volume, (region * 16 - HALF + 8 * j) % rows, 8, 1) for j in range(4)
    ]
    window = jnp.transpose(jnp.concatenate(pieces, axis=1), (1, 0, 2))
    slabs = lax.axis_size("zslab")
    lower = lax.ppermute(window, "zslab", [(s, s + 1) for s in range(slabs - 1)])
    upper = lax.ppermute(window, "zslab", [(s + 1, s) for s in range(slabs - 1)])
    high, low, scale = call(
        volume_kernel,
        (
            jax.ShapeDtypeStruct((NK, 48, NY), bf16),
            jax.ShapeDtypeStruct((NK, 48, NY), bf16),
            jax.ShapeDtypeStruct((STRIP, SLAB, NY), f32),
        ),
        [pltpu.VMEM((NK, 48, NY), f32)],
        (place, lower, window, upper), [SMEM] + [VMEM] * 3, 1 << 24, 1 << 21,
    )
    spread = jnp.asarray(spread_table(), bf16)
    strip = jax.ShapeDtypeStruct((STRIP, SLAB, NY), f32)
    parts = call(
        score_kernel, (strip,) * 4,
        [
            pltpu.VMEM((KDIM // LANES, NO * TS, LANES), f32),
            pltpu.VMEM((NK, 2, NO, KDIM), f32),
            pltpu.VMEM((NK, 2, NO, KDIM), bf16),
            pltpu.VMEM((NK, 2, NO, KDIM), bf16),
            pltpu.VMEM((512, KDIM), bf16),
            pltpu.VMEM((KDIM, NY), bf16),
            pltpu.VMEM((KDIM, NY), bf16),
            pltpu.VMEM((NK, 256, NY), f32),
            pltpu.VMEM((NF // 2, SLAB, NY), f32),
        ],
        (place, *gathered, spread, high, low), [SMEM] + [VMEM] * 7, 1 << 33, 1 << 21,
    )
    arrived = [parts[0]] + [swap(parts[m], m) for m in range(1, GROUP)]
    return call(
        last_kernel, jax.ShapeDtypeStruct((SLAB, STRIP, NY), f32), [],
        (scale, *arrived), [VMEM] * 5, 1 << 16, 1 << 18,
    )


def solution(mesh):
    return jax.shard_map(
        shards,
        mesh=mesh,
        in_specs=(P("zslab", None, None), P("orient", None, None, None), P()),
        out_specs=P("zslab", "orient", None),
        check_vma=False,
    )
```

time: 1370 us -> 61.8 us (0.05)
  waiting for transfers between devices: 1190 us -> 15.2 us
  matrix products: 130 us -> 0 us
  starting transfers between devices: 7.28 us -> 25.5 us
  Pallas kernels: 0 us -> 18 us
  between operations: 15.3 us -> 0.25 us
    pmax x1 -> x0, waiting for transfers between devices: 608 us -> none  [shards(): whole = lax.pmax(score, 'orient')]
    all_gather x2 -> x0, waiting for transfers between devices: 562 us -> none  [the longest x1 307 us: shards(): lax.all_gather(vol_real, 'orient', axis=1, tiled=True)]
    dot_general x49 -> x0, matrix products: 129 us -> none  [matmul_axis(): jnp.einsum(forms[axis], matrix, field, precision=lax.Precision.HIGHEST)]
    ppermute x2 -> x11, starting transfers between devices: 7.19 us -> 25.5 us  [the longest x9 18.5 us: swap(): return lax.ppermute(value, 'orient', [(i, i ^ mask) for i in range(count)])]
    pallas_call x0 -> x4, Pallas kernels: none -> 18 us  [call(): pl.pallas_call(kernel, out_shape=outs, in_specs=specs, out_specs=[VMEM] *...]
  transfers between devices with their start and end apart: 5 -> 11, of which waited for: 4 -> 7; matrix products, arithmetic and copies ran while one was open for 4% -> 2% of each run, Pallas kernels for 0% -> 4%
where the time goes in v1:
time: 61.8 us; the launch traced here: 61.6 us
  starting transfers between devices  25.5 us (41%)
  Pallas kernels  18 us (29%)
  waiting for transfers between devices  15.2 us (25%)
  local copies, waits for them, and re-layouts  1.8 us (3%)
  other arithmetic  0.94 us (2%)
    ppermute x9, starting transfers between devices, swap(): return lax.ppermute(value, 'orient', [(i, i ^ mask) for i in range(count)])  18.5 us
    pallas_call x4, Pallas kernels, call(): pl.pallas_call(kernel, out_shape=outs, in_specs=specs, out_specs=[VMEM] *...  18 us
    ppermute x9, waiting for transfers between devices, swap(): return lax.ppermute(value, 'orient', [(i, i ^ mask) for i in range(count)])  15.2 us
    ppermute x1, starting transfers between devices, shards(): lax.ppermute(window, 'zslab', [(s + 1, s) for s in range(slabs - 1)])  5.15 us
    ppermute x1, starting transfers between devices, shards(): lax.ppermute(window, 'zslab', [(s, s + 1) for s in range(slabs - 1)])  1.92 us
  transfers between devices with their start and end apart: 11, of which 7 were waited for; matrix products, arithmetic and copies ran while one was open for 2% of the time, Pallas kernels for 4%

profile of v1, /device:TPU:4, one launch (start us, length us, event | category | flops | bytes accessed | tf_op | source)
XLA Modules:
  0.0 61.6 jit_solution(7414079071679779442)
XLA Ops:
  0.1 0.0 copy-start.3
  0.1 1.2 %constant_dynamic-slice_fusion.3 = (f32[8,8,256]{2,1,0:T(8,128)S(1)}, f32[8,8,256]{2,1,0:T(8,128)S(1)}, f32[8,8,256]{2,1,0:T(8,128)S(1)}, f32[8,8,256]{2,1,0:T(8,128)S(1)}) fusion(f32[8,256,256]{2,1,0:T(8,128)} %param.7, s32[]{:T(128)S(6)} %select_n.42, s32[]{:T(128)S(6)} %select_n.46, s32[]{:T(128)S(6)} %select_n.44, s32[]{:T(128)S(6)} %select_n.48), kind=kLoop, calls=%fused_computation.6 | loop fusion | bytes 524304 | tf_op jit(solution)/shard_map/dynamic_slice | solution.py:296
  1.5 1.9 %collective-permute-start = (f32[32,8,256]{2,1,0:T(8,128)S(1)}, f32[32,8,256]{2,1,0:T(8,128)S(1)}, u32[]{:S(2)}, u32[]{:S(2)}) collective-permute-start(f32[32,8,256]{2,1,0:T(8,128)S(1)} %maximum_bitcast_fusion.own_ref), channel_id=1, source_target_pairs={{0,1},{1,2},{2,3},{4,5},{5,6},{6,7},{8,9},{9,10},{10,11},{12,13},{... | collective-permute-start | bytes 786440 | tf_op jit(solution)/shard_map/ppermute | solution.py:300
  3.4 5.1 %collective-permute-start.1 = (f32[32,8,256]{2,1,0:T(8,128)S(1)}, f32[32,8,256]{2,1,0:T(8,128)S(1)}, u32[]{:S(2)}, u32[]{:S(2)}) collective-permute-start(f32[32,8,256]{2,1,0:T(8,128)S(1)} %maximum_bitcast_fusion.own_ref), channel_id=1, source_target_pairs={{1,0},{2,1},{3,2},{5,4},{6,5},{7,6},{9,8},{10,9},{11,10},{13,12},{... | collective-permute-start | bytes 786440 | tf_op jit(solution)/shard_map/ppermute | solution.py:301
  8.6 0.9 %convert_bitcast_fusion = f32[16,16,16]{1,0,2:T(8,128)S(1)} fusion(s32[16,16,16]{2,1,0:T(8,128)} %param.9), kind=kLoop, calls=%fused_computation.1 | loop fusion | flops 4096 | bytes 32768 | tf_op jit(solution)/shard_map/transpose | solution.py:286
  9.5 0.1 copy.13
  9.6 0.1 reshape.11.wedge_ref
  9.8 0.1 copy.12
  9.9 0.1 reshape.10.template_ref
  10.0 1.6 %shard_map.74 = f32[16,256]{1,0:T(8,128)S(1)} custom-call(f32[16,256]{1,0:T(8,128)S(1)} %reshape.10.template_ref, f32[16,256]{1,0:T(8,128)S(1)} %reshape.11.wedge_ref, f32[256,512]{1,0:T(8,128)S(1)} %copy-done, f32[32,32]{1,0:T(8,128)S(1)} %copy-done.1, f32[32,32]{1,0:T(8,128)S(1)} %copy-done.2), custom_call_target="tpu_custom_call" | custom-call | flops 4194304 | bytes 1048576 | tf_op jit(solution)/shard_map/pallas_call | solution.py:264
  11.6 7.3 %collective-permute-start.2 = (f32[16,256]{1,0:T(8,128)S(1)}, f32[16,256]{1,0:T(8,128)S(1)}, u32[]{:S(2)}, u32[]{:S(2)}) collective-permute-start(f32[16,256]{1,0:T(8,128)S(1)} %shard_map.74), channel_id=1, source_target_pairs={{0,16},{4,20},{8,24},{12,28},{16,0},{20,4},{24,8},{28,12},{32,48},... | collective-permute-start | bytes 49160 | tf_op jit(solution)/shard_map/ppermute | solution.py:283
  18.9 3.2 %collective-permute-start.3 = (f32[16,256]{1,0:T(8,128)S(1)}, f32[16,256]{1,0:T(8,128)S(1)}, u32[]{:S(2)}, u32[]{:S(2)}) collective-permute-start(f32[16,256]{1,0:T(8,128)S(1)} %shard_map.74), channel_id=1, source_target_pairs={{0,64},{4,68},{8,72},{12,76},{16,80},{20,84},{24,88},{28,92},{32,9... | collective-permute-start | bytes 49160 | tf_op jit(solution)/shard_map/ppermute | solution.py:283
  22.1 0.0 collective-permute-start.4
  22.1 0.0 collective-permute-done.2
  22.1 2.0 %collective-permute-done.3 = f32[16,256]{1,0:T(8,128)S(1)} collective-permute-done((f32[16,256]{1,0:T(8,128)S(1)}, f32[16,256]{1,0:T(8,128)S(1)}, u32[]{:S(2)}, u32[]{:S(2)}) %collective-permute-start.3) | collective-permute-done | bytes 16416 | tf_op jit(solution)/shard_map/ppermute | solution.py:283
  24.1 8.0 %collective-permute-done.4 = f32[16,256]{1,0:T(8,128)S(1)} collective-permute-done((f32[16,256]{1,0:T(8,128)S(1)}, f32[16,256]{1,0:T(8,128)S(1)}, u32[]{:S(2)}, u32[]{:S(2)}) %collective-permute-start.4) | collective-permute-done | bytes 16416 | tf_op jit(solution)/shard_map/ppermute | solution.py:283
  32.1 0.7 %collective-permute-start.5 = (f32[64,256]{1,0:T(8,128)S(1)}, f32[64,256]{1,0:T(8,128)S(1)}, u32[]{:S(2)}, u32[]{:S(2)}) collective-permute-start(f32[64,256]{1,0:T(8,128)S(1)} %pad_maximum_fusion.a_ref), channel_id=1, source_target_pairs={{0,32},{4,36},{8,40},{12,44},{16,48},{20,52},{24,56},{28,60},{32,0... | collective-permute-start | bytes 196616 | tf_op jit(solution)/shard_map/ppermute | solution.py:283
  32.8 1.2 %collective-permute-start.6 = (f32[64,256]{1,0:T(8,128)S(1)}, f32[64,256]{1,0:T(8,128)S(1)}, u32[]{:S(2)}, u32[]{:S(2)}) collective-permute-start(f32[64,256]{1,0:T(8,128)S(1)} %pad_maximum_fusion.a_ref), channel_id=1, source_target_pairs={{0,128},{4,132},{8,136},{12,140},{16,144},{20,148},{24,152},{28,15... | collective-permute-start | bytes 196616 | tf_op jit(solution)/shard_map/ppermute | solution.py:283
  34.0 1.6 %collective-permute-start.7 = (f32[64,256]{1,0:T(8,128)S(1)}, f32[64,256]{1,0:T(8,128)S(1)}, u32[]{:S(2)}, u32[]{:S(2)}) collective-permute-start(f32[64,256]{1,0:T(8,128)S(1)} %pad_maximum_fusion.a_ref), channel_id=1, source_target_pairs={{0,160},{4,164},{8,168},{12,172},{16,176},{20,180},{24,184},{28,18... | collective-permute-start | bytes 196616 | tf_op jit(solution)/shard_map/ppermute | solution.py:283
  35.6 0.0 collective-permute-done.lower_ref
  35.6 0.0 collective-permute-done.1.upper_ref
  35.6 0.9 %shard_map.73 = (bf16[16,48,256]{2,1,0:T(8,128)(2,1)S(1)}, bf16[16,48,256]{2,1,0:T(8,128)(2,1)S(1)}, f32[4,8,256]{2,1,0:T(8,128)S(1)}) custom-call(s32[1]{0:T(128)} %bitcast.place_ref, f32[32,8,256]{2,1,0:T(8,128)S(1)} %collective-permute-done.lower_ref, f32[32,8,256]{2,1,0:T(8,128)S(1)} %maximum_bitcast_fusion.own_ref, ...), custom_call_target="tpu_custom_call" | custom-call | flops 16777216 | bytes 2097152 | tf_op jit(solution)/shard_map/pallas_call | solution.py:264
  36.5 0.6 collective-permute-done.6.c_ref
  37.1 2.1 %collective-permute-done.7.d_ref = f32[64,256]{1,0:T(8,128)S(1)} collective-permute-done((f32[64,256]{1,0:T(8,128)S(1)}, f32[64,256]{1,0:T(8,128)S(1)}, u32[]{:S(2)}, u32[]{:S(2)}) %collective-permute-start.7) | collective-permute-done | bytes 65568 | tf_op jit(solution)/shard_map/ppermute | solution.py:283
  39.2 14.9 %shard_map.75 = (f32[4,8,256]{2,1,0:T(8,128)S(1)}, f32[4,8,256]{2,1,0:T(8,128)S(1)}, f32[4,8,256]{2,1,0:T(8,128)S(1)}, f32[4,8,256]{2,1,0:T(8,128)S(1)}) custom-call(s32[1]{0:T(128)} %bitcast.place_ref, f32[64,256]{1,0:T(8,128)S(1)} %pad_maximum_fusion.a_ref, f32[64,256]{1,0:T(8,128)S(1)} %collective-permute-done.5.b_ref, ...), custom_call_target="tpu_custom_call" | custom-call | flops 8589934592 | bytes 2097152 | tf_op jit(solution)/shard_map/pallas_call | solution.py:264
  54.1 2.0 %collective-permute-start.10 = (f32[4,8,256]{2,1,0:T(8,128)S(1)}, f32[4,8,256]{2,1,0:T(8,128)S(1)}, u32[]{:S(2)}, u32[]{:S(2)}) collective-permute-start(f32[4,8,256]{2,1,0:T(8,128)S(1)} %get-tuple-element.18), channel_id=1, source_target_pairs={{0,12},{4,8},{8,4},{12,0},{16,28},{20,24},{24,20},{28,16},{32,44},... | collective-permute-start | bytes 98312 | tf_op jit(solution)/shard_map/ppermute | solution.py:283
  56.1 0.1 collective-permute-start.8
  56.2 2.4 %collective-permute-start.9 = (f32[4,8,256]{2,1,0:T(8,128)S(1)}, f32[4,8,256]{2,1,0:T(8,128)S(1)}, u32[]{:S(2)}, u32[]{:S(2)}) collective-permute-start(f32[4,8,256]{2,1,0:T(8,128)S(1)} %get-tuple-element.17), channel_id=1, source_target_pairs={{0,8},{4,12},{8,0},{12,4},{16,24},{20,28},{24,16},{28,20},{32,40},... | collective-permute-start | bytes 98312 | tf_op jit(solution)/shard_map/ppermute | solution.py:283
  58.5 1.3 %collective-permute-done.10.d_ref = f32[4,8,256]{2,1,0:T(8,128)S(1)} collective-permute-done((f32[4,8,256]{2,1,0:T(8,128)S(1)}, f32[4,8,256]{2,1,0:T(8,128)S(1)}, u32[]{:S(2)}, u32[]{:S(2)}) %collective-permute-start.10) | collective-permute-done | bytes 32800 | tf_op jit(solution)/shard_map/ppermute | solution.py:283
  59.9 0.3 collective-permute-done.8.b_ref
  60.2 0.8 %collective-permute-done.9.c_ref = f32[4,8,256]{2,1,0:T(8,128)S(1)} collective-permute-done((f32[4,8,256]{2,1,0:T(8,128)S(1)}, f32[4,8,256]{2,1,0:T(8,128)S(1)}, u32[]{:S(2)}, u32[]{:S(2)}) %collective-permute-start.9) | collective-permute-done | bytes 32800 | tf_op jit(solution)/shard_map/ppermute | solution.py:283
  61.0 0.6 %shard_map.76 = f32[8,4,256]{2,1,0:T(4,128)} custom-call(f32[4,8,256]{2,1,0:T(8,128)S(1)} %get-tuple-element.12.scale_ref, f32[4,8,256]{2,1,0:T(8,128)S(1)} %get-tuple-element.15.a_ref, f32[4,8,256]{2,1,0:T(8,128)S(1)} %collective-permute-done.8.b_ref, f32[4,8,256]{2,1,0:T(8,128)S(1)} %collective-permute-done.9.c_ref, ...), custom_call_target="tpu_custom_call" | custom-call | flops 65536 | bytes 262144 | tf_op jit(solution)/shard_map/pallas_call | solution.py:264
  (16 shorter events, 0.1 us)
Async XLA Ops:
  0.0 10.0 %copy-start = (f32[256,512]{1,0:T(8,128)S(1)}, f32[256,512]{1,0:T(8,128)}, u32[]{:S(2)}) copy-start(f32[256,512]{1,0:T(8,128)} %constant.73.clone.right_ref) | copy-start | bytes 1572868
  0.0 10.0 %copy-start.1 = (f32[32,32]{1,0:T(8,128)S(1)}, f32[32,32]{1,0:T(8,128)}, u32[]{:S(2)}) copy-start(f32[32,32]{1,0:T(8,128)} %constant.74.clone.ahead_ref) | copy-start | bytes 12292
  0.0 10.0 %copy-start.2 = (f32[32,32]{1,0:T(8,128)S(1)}, f32[32,32]{1,0:T(8,128)}, u32[]{:S(2)}) copy-start(f32[32,32]{1,0:T(8,128)} %constant.75.clone.back_ref) | copy-start | bytes 12292
  0.0 9.7 %copy-start.4 = (f32[1,16,16,16]{3,2,1,0:T(8,128)S(1)}, f32[1,16,16,16]{3,2,1,0:T(8,128)}, u32[]{:S(2)}) copy-start(f32[1,16,16,16]{3,2,1,0:T(8,128)} %param.8) | copy-start | bytes 49156
  0.1 39.0 %copy-start.3 = (bf16[256,768]{1,0:T(8,128)(2,1)S(1)}, bf16[256,768]{1,0:T(8,128)(2,1)}, u32[]{:S(2)}) copy-start(bf16[256,768]{1,0:T(8,128)(2,1)} %constant.76.clone.spread_ref) | copy-start | bytes 1179652
  1.5 34.1 %collective-permute-start = (f32[32,8,256]{2,1,0:T(8,128)S(1)}, f32[32,8,256]{2,1,0:T(8,128)S(1)}, u32[]{:S(2)}, u32[]{:S(2)}) collective-permute-start(f32[32,8,256]{2,1,0:T(8,128)S(1)} %maximum_bitcast_fusion.own_ref), channel_id=1, source_target_pairs={{0,1},{1,2},{2,3},{4,5},{5,6},{6,7},{8,9},{9,10},{10,11},{12,13},{... | collective-permute-start | bytes 786440 | tf_op jit(solution)/shard_map/ppermute | solution.py:300
  3.4 32.2 %collective-permute-start.1 = (f32[32,8,256]{2,1,0:T(8,128)S(1)}, f32[32,8,256]{2,1,0:T(8,128)S(1)}, u32[]{:S(2)}, u32[]{:S(2)}) collective-permute-start(f32[32,8,256]{2,1,0:T(8,128)S(1)} %maximum_bitcast_fusion.own_ref), channel_id=1, source_target_pairs={{1,0},{2,1},{3,2},{5,4},{6,5},{7,6},{9,8},{10,9},{11,10},{13,12},{... | collective-permute-start | bytes 786440 | tf_op jit(solution)/shard_map/ppermute | solution.py:301
  11.6 10.5 %collective-permute-start.2 = (f32[16,256]{1,0:T(8,128)S(1)}, f32[16,256]{1,0:T(8,128)S(1)}, u32[]{:S(2)}, u32[]{:S(2)}) collective-permute-start(f32[16,256]{1,0:T(8,128)S(1)} %shard_map.74), channel_id=1, source_target_pairs={{0,16},{4,20},{8,24},{12,28},{16,0},{20,4},{24,8},{28,12},{32,48},... | collective-permute-start | bytes 49160 | tf_op jit(solution)/shard_map/ppermute | solution.py:283
  18.9 5.2 %collective-permute-start.3 = (f32[16,256]{1,0:T(8,128)S(1)}, f32[16,256]{1,0:T(8,128)S(1)}, u32[]{:S(2)}, u32[]{:S(2)}) collective-permute-start(f32[16,256]{1,0:T(8,128)S(1)} %shard_map.74), channel_id=1, source_target_pairs={{0,64},{4,68},{8,72},{12,76},{16,80},{20,84},{24,88},{28,92},{32,9... | collective-permute-start | bytes 49160 | tf_op jit(solution)/shard_map/ppermute | solution.py:283
  22.1 10.0 %collective-permute-start.4 = (f32[16,256]{1,0:T(8,128)S(1)}, f32[16,256]{1,0:T(8,128)S(1)}, u32[]{:S(2)}, u32[]{:S(2)}) collective-permute-start(f32[16,256]{1,0:T(8,128)S(1)} %shard_map.74), channel_id=1, source_target_pairs={{0,80},{4,84},{8,88},{12,92},{16,64},{20,68},{24,72},{28,76},{32,1... | collective-permute-start | bytes 49160 | tf_op jit(solution)/shard_map/ppermute | solution.py:283
  32.1 4.4 %collective-permute-start.5 = (f32[64,256]{1,0:T(8,128)S(1)}, f32[64,256]{1,0:T(8,128)S(1)}, u32[]{:S(2)}, u32[]{:S(2)}) collective-permute-start(f32[64,256]{1,0:T(8,128)S(1)} %pad_maximum_fusion.a_ref), channel_id=1, source_target_pairs={{0,32},{4,36},{8,40},{12,44},{16,48},{20,52},{24,56},{28,60},{32,0... | collective-permute-start | bytes 196616 | tf_op jit(solution)/shard_map/ppermute | solution.py:283
  32.8 4.3 %collective-permute-start.6 = (f32[64,256]{1,0:T(8,128)S(1)}, f32[64,256]{1,0:T(8,128)S(1)}, u32[]{:S(2)}, u32[]{:S(2)}) collective-permute-start(f32[64,256]{1,0:T(8,128)S(1)} %pad_maximum_fusion.a_ref), channel_id=1, source_target_pairs={{0,128},{4,132},{8,136},{12,140},{16,144},{20,148},{24,152},{28,15... | collective-permute-start | bytes 196616 | tf_op jit(solution)/shard_map/ppermute | solution.py:283
  34.0 5.2 %collective-permute-start.7 = (f32[64,256]{1,0:T(8,128)S(1)}, f32[64,256]{1,0:T(8,128)S(1)}, u32[]{:S(2)}, u32[]{:S(2)}) collective-permute-start(f32[64,256]{1,0:T(8,128)S(1)} %pad_maximum_fusion.a_ref), channel_id=1, source_target_pairs={{0,160},{4,164},{8,168},{12,172},{16,176},{20,180},{24,184},{28,18... | collective-permute-start | bytes 196616 | tf_op jit(solution)/shard_map/ppermute | solution.py:283
  54.1 5.8 %collective-permute-start.10 = (f32[4,8,256]{2,1,0:T(8,128)S(1)}, f32[4,8,256]{2,1,0:T(8,128)S(1)}, u32[]{:S(2)}, u32[]{:S(2)}) collective-permute-start(f32[4,8,256]{2,1,0:T(8,128)S(1)} %get-tuple-element.18), channel_id=1, source_target_pairs={{0,12},{4,8},{8,4},{12,0},{16,28},{20,24},{24,20},{28,16},{32,44},... | collective-permute-start | bytes 98312 | tf_op jit(solution)/shard_map/ppermute | solution.py:283
  56.1 4.1 %collective-permute-start.8 = (f32[4,8,256]{2,1,0:T(8,128)S(1)}, f32[4,8,256]{2,1,0:T(8,128)S(1)}, u32[]{:S(2)}, u32[]{:S(2)}) collective-permute-start(f32[4,8,256]{2,1,0:T(8,128)S(1)} %get-tuple-element.16), channel_id=1, source_target_pairs={{0,4},{4,0},{8,12},{12,8},{16,20},{20,16},{24,28},{28,24},{32,36},... | collective-permute-start | bytes 98312 | tf_op jit(solution)/shard_map/ppermute | solution.py:283
  56.2 4.8 %collective-permute-start.9 = (f32[4,8,256]{2,1,0:T(8,128)S(1)}, f32[4,8,256]{2,1,0:T(8,128)S(1)}, u32[]{:S(2)}, u32[]{:S(2)}) collective-permute-start(f32[4,8,256]{2,1,0:T(8,128)S(1)} %get-tuple-element.17), channel_id=1, source_target_pairs={{0,8},{4,12},{8,0},{12,4},{16,24},{20,28},{24,16},{28,20},{32,40},... | collective-permute-start | bytes 98312 | tf_op jit(solution)/shard_map/ppermute | solution.py:283

commit v2 on v1

--- a/solution.py
+++ b/solution.py
@@ -116,11 +116,12 @@
 
 
 def spread_table():
-    out = np.zeros((TS, TS, TS, 48), np.float32)
-    for b in range(TS):
-        for c in range(TS):
-            out[b, c, b, c] = 1.0
-    return out.reshape(TS * TS, KDIM)
+    out = np.zeros((2, TS, TS, TS, 48), np.float32)
+    for part in range(2):
+        for b in range(TS):
+            for c in range(TS):
+                out[part, b, c, b, 24 * part + c] = 1.0
+    return out.reshape(2 * TS * TS, KDIM)
 
 
 def filter_kernel(template_ref, wedge_ref, right_ref, ahead_ref, back_ref, out_ref):
@@ -136,16 +137,20 @@
     filt = product(spec[:TS], right_ref[:, :width]) + product(spec[TS:], right_ref[:, width:])
     filt = filt * (1.0 / float(TS**3))
     centered = filt - jnp.sum(filt) * (1.0 / float(TS**3))
-    out_ref[...] = centered / jnp.sqrt(jnp.sum(centered * centered) + 1e-05)
-
-
-def volume_kernel(place_ref, lower_ref, own_ref, upper_ref, high_ref, low_ref, scale_ref, spec_ref):
-    for block, ref in enumerate((lower_ref, own_ref, upper_ref)):
+    normed = centered / jnp.sqrt(jnp.sum(centered * centered) + 1e-05)
+    out_ref[...] = jnp.concatenate([normed[:, :LANES], normed[:, LANES:]], axis=0)
+
+
+def volume_kernel(place_ref, inside_ref, own_ref, across_ref, high_ref, low_ref, scale_ref, spec_ref):
+    even = place_ref[1] % 2 == 0
+    inside_at = pl.multiple_of(jnp.where(even, 16, 0), 8)
+    across_at = pl.multiple_of(16 - inside_at, 8)
+    for ref, start in ((inside_ref, inside_at), (own_ref, 8), (across_ref, across_at)):
         for lane in range(0, NY, LANES):
             bins = forward([ref[x, :, lane : lane + LANES] for x in range(NF)])
             for k, (re, im) in enumerate(slots(bins)):
-                spec_ref[k, 8 * block : 8 * block + 8, lane : lane + LANES] = re
-                spec_ref[k, 24 + 8 * block : 32 + 8 * block, lane : lane + LANES] = im
+                spec_ref[k, pl.ds(start, 8), lane : lane + LANES] = re
+                spec_ref[k, pl.ds(start + 24, 8), lane : lane + LANES] = im
 
     def split(k, carry):
         high_ref[k], low_ref[k] = halves(spec_ref[k])
@@ -155,7 +160,10 @@
     first = place_ref[0] * STRIP
     sums = []
     for x in range(STRIP + TS - 1):
-        layers = jnp.concatenate([r[first + x] for r in (lower_ref, own_ref, upper_ref)], axis=0)
+        inside, across = inside_ref[first + x], across_ref[first + x]
+        layers = jnp.concatenate(
+            [jnp.where(even, across, inside), own_ref[first + x], jnp.where(even, inside, across)], axis=0
+        )
         sums.append(layers * layers)
     for step in (1, 2, 4, 8):
         sums = [sums[i] + sums[i + step] for i in range(len(sums) - step)]
@@ -171,59 +179,68 @@
 
 
 def score_kernel(
-    place_ref, a_ref, b_ref, c_ref, d_ref, spread_ref, high_ref, low_ref,
+    place_ref, a_ref, b_ref, spread_ref, high_ref, low_ref,
     out0_ref, out1_ref, out2_ref, out3_ref,
-    wide_ref, base_ref, base_high, base_low, left_ref, right_high, right_low, prod_ref, best_ref,
+    spec_ref, base_ref, left_a, left_b, high_a, high_b, low_a, low_b, prod_ref, best_ref,
 ):
-    for quarter, ref in enumerate((a_ref, b_ref, c_ref, d_ref)):
-        high, low = halves(ref[...])
-        rows = ref.shape[0]
-        wide = jnp.dot(
-            high, spread_ref[...], preferred_element_type=jnp.float32
-        ) + jnp.dot(low, spread_ref[...], preferred_element_type=jnp.float32)
-        for j in range(KDIM // LANES):
-            wide_ref[j, rows * quarter : rows * quarter + rows, :] = wide[:, j * LANES : (j + 1) * LANES]
-    for o in range(0, NO, 8):
-        for lane in range(0, KDIM, LANES):
-            rows = [
-                wide_ref[lane // LANES, pl.ds(o * TS + a, 8, stride=TS), :] for a in range(TS)
-            ]
-            bins = forward(rows + [None] * (NF - TS))
-            for k, (re, im) in enumerate(slots(bins)):
-                base_ref[k, 0, o : o + 8, lane : lane + LANES] = re
-                base_ref[k, 1, o : o + 8, lane : lane + LANES] = im
-
-    def assemble(k, carry):
-        re, im = base_ref[k, 0], base_ref[k, 1]
-        packed = (k == 0).astype(jnp.float32)
-        mixed = 1.0 - packed
-        first = re + mixed * pltpu.roll(im, 24, axis=1)
-        second = pltpu.roll(mixed * re + packed * im, 24, axis=1) - mixed * im
-        base_high[k, 0], base_low[k, 0] = halves(first)
-        base_high[k, 1], base_low[k, 1] = halves(second)
+    width = TS * TS
+    for lane in range(0, width, LANES):
+        start = lane // LANES * TS
+        groups = []
+        for ref in (a_ref, b_ref):
+            rows = [ref[pl.ds(start + a, 8, stride=2 * TS), :] for a in range(TS)]
+            groups.append(slots(forward(rows + [None] * (NF - TS))))
+        for k, ((re0, im0), (re1, im1)) in enumerate(zip(*groups)):
+            re = halves(jnp.concatenate([re0, re1], axis=0))
+            im = halves(jnp.concatenate([im0, im1], axis=0))
+            for h in range(2):
+                row, nil = 64 * k + 32 * h, jnp.zeros_like(re[h])
+                left, right = slice(lane, lane + LANES), slice(width + lane, width + lane + LANES)
+                spec_ref[row : row + NO, left] = re[h]
+                spec_ref[row : row + NO, right] = nil if k == 0 else im[h]
+                spec_ref[row + NO : row + 2 * NO, left] = nil if k == 0 else -im[h]
+                spec_ref[row + NO : row + 2 * NO, right] = im[h] if k == 0 else re[h]
+
+    def expand(i, carry):
+        row = pl.multiple_of(i * 256, 256)
+        base_ref[pl.ds(row, 256), :] = jnp.dot(
+            spec_ref[pl.ds(row, 256), :], spread_ref[...], preferred_element_type=jnp.float32
+        ).astype(jnp.bfloat16)
         return carry
 
-    lax.fori_loop(0, NK, assemble, 0)
-
-    def one(k, carry):
-        for part in range(2):
-            for row0, ref in ((0, base_high), (256, base_low)):
-                value = ref[k, part]
+    lax.fori_loop(0, 4, expand, 0)
+
+    def build(k, left, right_high, right_low):
+        for h in range(2):
+            for part in range(2):
+                at = pl.multiple_of(k * 64 + 32 * h + 16 * part, 16)
+                value = base_ref[pl.ds(at, NO), :]
                 for z in range(SLAB):
-                    at = row0 + part * 128 + z * NO
-                    left_ref[at : at + NO, :] = value if z == 0 else pltpu.roll(value, z, axis=1)
+                    row = h * 256 + part * 128 + z * NO
+                    left[row : row + NO, :] = value if z == 0 else pltpu.roll(value, z, axis=1)
         for src, dst in ((high_ref, right_high), (low_ref, right_low)):
             value = src[k]
             for b in range(TS):
                 shift = (HALF - b) % NY
                 dst[48 * b : 48 * b + 48, :] = value if shift == 0 else pltpu.roll(value, shift, axis=1)
-        both = jnp.dot(left_ref[...], right_high[...], preferred_element_type=jnp.float32)
-        low = jnp.dot(left_ref[:256], right_low[...], preferred_element_type=jnp.float32)
+
+    def multiply(k, left, right_high, right_low):
+        both = jnp.dot(left[...], right_high[...], preferred_element_type=jnp.float32)
+        low = jnp.dot(left[:256], right_low[...], preferred_element_type=jnp.float32)
         prod_ref[k] = both[:256] + (both[256:] + low)
+
+    first, second = (left_a, high_a, low_a), (left_b, high_b, low_b)
+    build(0, *first)
+
+    def two(i, carry):
+        k = 2 * i
+        multiply(k, *first)
+        build(k + 1, *second)
+        multiply(k + 1, *second)
+        build(jnp.minimum(k + 2, NK - 1), *first)
         return carry
 
-    lax.fori_loop(0, NK, one, 0)
-
+    lax.fori_loop(0, NK // 2, two, 0)
     best_ref[...] = jnp.zeros_like(best_ref)
 
     def finish(z, carry):
@@ -276,7 +293,7 @@
     f32, bf16 = jnp.float32, jnp.bfloat16
     count = lax.axis_size("orient")
     me = lax.axis_index("orient")
-    place = (me % GROUP).astype(jnp.int32).reshape(1)
+    place = jnp.stack([me % GROUP, lax.axis_index("zslab")]).astype(jnp.int32)
     region = me // GROUP
 
     def swap(value, mask):
@@ -285,11 +302,14 @@
     template = jnp.transpose(templates[0], (1, 2, 0)).reshape(TS, TS * TS)
     keep = jnp.transpose(wedge.astype(f32), (1, 2, 0)).reshape(TS, TS * TS)
     normed = call(
-        filter_kernel, jax.ShapeDtypeStruct((TS, TS * TS), f32), [],
+        filter_kernel, jax.ShapeDtypeStruct((2 * TS, LANES), f32), [],
         (template, keep) + filter_tables(), [VMEM] * 5, 1 << 22, 1 << 20,
     )
-    four = jnp.concatenate([normed] + [swap(normed, m) for m in (4, 16, 20)], axis=0)
-    gathered = [four] + [swap(four, m) for m in (8, 32, 40)]
+    near = [[8 * a + b for a in range(8)] for b in range(8)]
+    eight = lax.all_to_all(
+        jnp.broadcast_to(normed, (8, 2 * TS, LANES)), "orient", 0, 0, tiled=True, axis_index_groups=near
+    ).reshape(16 * TS, LANES)
+    gathered = [eight, swap(eight, 4)]
 
     rows = volume.shape[1]
     pieces = [
@@ -297,8 +317,8 @@
     ]
     window = jnp.transpose(jnp.concatenate(pieces, axis=1), (1, 0, 2))
     slabs = lax.axis_size("zslab")
-    lower = lax.ppermute(window, "zslab", [(s, s + 1) for s in range(slabs - 1)])
-    upper = lax.ppermute(window, "zslab", [(s + 1, s) for s in range(slabs - 1)])
+    inside = lax.ppermute(window, "zslab", [(s, s ^ 1) for s in range(slabs)])
+    across = lax.ppermute(window, "zslab", [(1, 2), (2, 1)])
     high, low, scale = call(
         volume_kernel,
         (
@@ -307,24 +327,25 @@
             jax.ShapeDtypeStruct((STRIP, SLAB, NY), f32),
         ),
         [pltpu.VMEM((NK, 48, NY), f32)],
-        (place, lower, window, upper), [SMEM] + [VMEM] * 3, 1 << 24, 1 << 21,
+        (place, inside, window, across), [SMEM] + [VMEM] * 3, 1 << 24, 1 << 21,
     )
     spread = jnp.asarray(spread_table(), bf16)
     strip = jax.ShapeDtypeStruct((STRIP, SLAB, NY), f32)
     parts = call(
         score_kernel, (strip,) * 4,
         [
-            pltpu.VMEM((KDIM // LANES, NO * TS, LANES), f32),
-            pltpu.VMEM((NK, 2, NO, KDIM), f32),
-            pltpu.VMEM((NK, 2, NO, KDIM), bf16),
-            pltpu.VMEM((NK, 2, NO, KDIM), bf16),
+            pltpu.VMEM((NK * 64, 2 * TS * TS), bf16),
+            pltpu.VMEM((NK * 64, KDIM), bf16),
             pltpu.VMEM((512, KDIM), bf16),
+            pltpu.VMEM((512, KDIM), bf16),
+            pltpu.VMEM((KDIM, NY), bf16),
+            pltpu.VMEM((KDIM, NY), bf16),
             pltpu.VMEM((KDIM, NY), bf16),
             pltpu.VMEM((KDIM, NY), bf16),
             pltpu.VMEM((NK, 256, NY), f32),
             pltpu.VMEM((NF // 2, SLAB, NY), f32),
         ],
-        (place, *gathered, spread, high, low), [SMEM] + [VMEM] * 7, 1 << 33, 1 << 21,
+        (place, *gathered, spread, high, low), [SMEM] + [VMEM] * 5, 1 << 33, 1 << 21,
     )
     arrived = [parts[0]] + [swap(parts[m], m) for m in range(1, GROUP)]
     return call(

time: 61.8 us -> 51.7 us (0.84)
  blocking collectives: 0 us -> 10.8 us
  starting transfers between devices: 25.5 us -> 15.9 us
  waiting for transfers between devices: 15.2 us -> 6.89 us
  Pallas kernels: 18 us -> 14.9 us
    all_to_all x0 -> x1, blocking collectives: none -> 10.8 us  [shards(): lax.all_to_all(jnp.broadcast_to(normed, (8, 2 * TS, LANES)), 'orient', 0,...]
    ppermute x9 -> x4, waiting for transfers between devices: 15.2 us -> 6.88 us  [swap(): return lax.ppermute(value, 'orient', [(i, i ^ mask) for i in range(count)])]
    ppermute x9 -> x4, starting transfers between devices: 18.5 us -> 11.7 us  [swap(): return lax.ppermute(value, 'orient', [(i, i ^ mask) for i in range(count)])]
    pallas_call x4, Pallas kernels: 18 us -> 14.9 us  [call(): pl.pallas_call(kernel, out_shape=outs, in_specs=specs, out_specs=[VMEM] *...]
    ppermute x2, starting transfers between devices: 7.07 us -> 4.21 us  [the longest x1 4.12 us: shards(): across = lax.ppermute(window, 'zslab', [(1, 2), (2, 1)])]
  transfers between devices with their start and end apart: 11 -> 6, of which waited for: 7 -> 3; matrix products, arithmetic and copies ran while one was open for 2% -> 3% of each run, Pallas kernels for 4% -> 6%
where the time goes in v2:
time: 51.7 us; the launch traced here: 51.5 us
  starting transfers between devices  15.9 us (31%)
  Pallas kernels  14.9 us (29%)
  blocking collectives  10.8 us (21%)
  waiting for transfers between devices  6.89 us (13%)
  local copies, waits for them, and re-layouts  1.78 us (3%)
  other arithmetic  1.01 us (2%)
    pallas_call x4, Pallas kernels, call(): pl.pallas_call(kernel, out_shape=outs, in_specs=specs, out_specs=[VMEM] *...  14.9 us
    ppermute x4, starting transfers between devices, swap(): return lax.ppermute(value, 'orient', [(i, i ^ mask) for i in range(count)])  11.7 us
    all_to_all x1, blocking collectives, shards(): lax.all_to_all(jnp.broadcast_to(normed, (8, 2 * TS, LANES)), 'orient', 0,...  10.8 us
    ppermute x4, waiting for transfers between devices, swap(): return lax.ppermute(value, 'orient', [(i, i ^ mask) for i in range(count)])  6.88 us
    ppermute x1, starting transfers between devices, shards(): across = lax.ppermute(window, 'zslab', [(1, 2), (2, 1)])  4.12 us
    dynamic_slice x1, local copies, waits for them, and re-layouts, shards(): lax.dynamic_slice_in_dim(volume, (region * 16 - HALF + 8 * j) % rows, 8, 1)  1.21 us
  transfers between devices with their start and end apart: 6, of which 3 were waited for; matrix products, arithmetic and copies ran while one was open for 3% of the time, Pallas kernels for 6%

profile of v2, /device:TPU:4, one launch (start us, length us, event | category | flops | bytes accessed | tf_op | source)
XLA Modules:
  0.0 51.5 jit_solution(7379828055984237154)
XLA Ops:
  0.0 0.0 copy-start
  0.0 0.0 copy-start.4
  0.1 1.2 %constant_dynamic-slice_fusion.3 = (f32[8,8,256]{2,1,0:T(8,128)S(1)}, f32[8,8,256]{2,1,0:T(8,128)S(1)}, f32[8,8,256]{2,1,0:T(8,128)S(1)}, f32[8,8,256]{2,1,0:T(8,128)S(1)}) fusion(f32[8,256,256]{2,1,0:T(8,128)} %param.7, s32[]{:T(128)S(6)} %select_n.42, s32[]{:T(128)S(6)} %select_n.46, s32[]{:T(128)S(6)} %select_n.44, s32[]{:T(128)S(6)} %select_n.48), kind=kLoop, calls=%fused_computation.5 | loop fusion | bytes 524304 | tf_op jit(solution)/shard_map/dynamic_slice | solution.py:316
  1.3 0.0 copy-start.3
  1.5 0.1 collective-permute-start
  1.6 4.1 %collective-permute-start.1 = (f32[32,8,256]{2,1,0:T(8,128)S(1)}, f32[32,8,256]{2,1,0:T(8,128)S(1)}, u32[]{:S(2)}, u32[]{:S(2)}) collective-permute-start(f32[32,8,256]{2,1,0:T(8,128)S(1)} %maximum_bitcast_fusion.own_ref), channel_id=1, source_target_pairs={{1,2},{2,1},{5,6},{6,5},{9,10},{10,9},{13,14},{14,13},{17,18},{18,... | collective-permute-start | bytes 786440 | tf_op jit(solution)/shard_map/ppermute | solution.py:321
  5.7 0.9 %convert_bitcast_fusion = f32[16,16,16]{1,0,2:T(8,128)S(1)} fusion(s32[16,16,16]{2,1,0:T(8,128)} %param.9), kind=kLoop, calls=%fused_computation.1 | loop fusion | flops 4096 | bytes 32768 | tf_op jit(solution)/shard_map/transpose | solution.py:303
  6.6 0.1 copy.13
  6.8 0.1 reshape.10.wedge_ref
  6.9 0.0 copy-done.4
  6.9 0.1 copy.12
  7.0 0.1 reshape.9.template_ref
  7.1 0.0 copy-done
  7.1 0.0 copy-done.1
  7.1 0.0 copy-done.2
  7.1 1.6 %shard_map.74 = f32[32,128]{1,0:T(8,128)S(1)} custom-call(f32[16,256]{1,0:T(8,128)S(1)} %reshape.9.template_ref, f32[16,256]{1,0:T(8,128)S(1)} %reshape.10.wedge_ref, f32[256,512]{1,0:T(8,128)S(1)} %copy-done, f32[32,32]{1,0:T(8,128)S(1)} %copy-done.1, f32[32,32]{1,0:T(8,128)S(1)} %copy-done.2), custom_call_target="tpu_custom_call" | custom-call | flops 4194304 | bytes 1048576 | tf_op jit(solution)/shard_map/pallas_call | solution.py:281
  8.7 10.8 %all_to_all.5 = f32[8,32,128]{2,1,0:T(8,128)S(1)} all-to-all(f32[8,32,128]{2,1,0:T(8,128)S(1)} %broadcast_in_dim.3), channel_id=1, replica_groups={{0,32,64,96,128,160,192,224},{4,36,68,100,132,164,196,228},{8,40,72,104..., dimensions={0} | all-to-all | bytes 262144 | tf_op jit(solution)/shard_map/all_to_all | solution.py:309
  19.5 7.2 %collective-permute-start.2 = (f32[256,128]{1,0:T(8,128)S(1)}, f32[256,128]{1,0:T(8,128)S(1)}, u32[]{:S(2)}, u32[]{:S(2)}) collective-permute-start(f32[256,128]{1,0:T(8,128)S(1)} %bitcast.10), channel_id=1, source_target_pairs={{0,16},{4,20},{8,24},{12,28},{16,0},{20,4},{24,8},{28,12},{32,48},... | collective-permute-start | bytes 393224 | tf_op jit(solution)/shard_map/ppermute | solution.py:300
  26.7 0.1 pad_add_fusion.place_ref
  26.8 0.0 collective-permute-done.inside_ref
  26.8 0.0 collective-permute-done.1.across_ref
  26.8 1.4 %shard_map.73 = (bf16[16,48,256]{2,1,0:T(8,128)(2,1)S(1)}, bf16[16,48,256]{2,1,0:T(8,128)(2,1)S(1)}, f32[4,8,256]{2,1,0:T(8,128)S(1)}) custom-call(s32[2]{0:T(128)S(1)} %pad_add_fusion.place_ref, f32[32,8,256]{2,1,0:T(8,128)S(1)} %collective-permute-done.inside_ref, f32[32,8,256]{2,1,0:T(8,128)S(1)} %maximum_bitcast_fusion.own_ref, ...), custom_call_target="tpu_custom_call" | custom-call | flops 16777216 | bytes 2097152 | tf_op jit(solution)/shard_map/pallas_call | solution.py:281
  28.2 2.4 %collective-permute-done.2.b_ref = f32[256,128]{1,0:T(8,128)S(1)} collective-permute-done((f32[256,128]{1,0:T(8,128)S(1)}, f32[256,128]{1,0:T(8,128)S(1)}, u32[]{:S(2)}, u32[]{:S(2)}) %collective-permute-start.2) | collective-permute-done | bytes 131104 | tf_op jit(solution)/shard_map/ppermute | solution.py:300
  30.6 0.0 copy-done.3
  30.6 11.3 %shard_map.75 = (f32[4,8,256]{2,1,0:T(8,128)S(1)}, f32[4,8,256]{2,1,0:T(8,128)S(1)}, f32[4,8,256]{2,1,0:T(8,128)S(1)}, f32[4,8,256]{2,1,0:T(8,128)S(1)}) custom-call(s32[2]{0:T(128)S(1)} %pad_add_fusion.place_ref, f32[256,128]{1,0:T(8,128)S(1)} %bitcast.11, f32[256,128]{1,0:T(8,128)S(1)} %collective-permute-done.2.b_ref, bf16[512,768]{1,0:T(8,128)(2,1)S(1)} %copy-done.3, ...), custom_call_target="tpu_custom_call" | custom-call | flops 8589934592 | bytes 2097152 | tf_op jit(solution)/shard_map/pallas_call | solution.py:281
  41.9 1.1 %collective-permute-start.3 = (f32[4,8,256]{2,1,0:T(8,128)S(1)}, f32[4,8,256]{2,1,0:T(8,128)S(1)}, u32[]{:S(2)}, u32[]{:S(2)}) collective-permute-start(f32[4,8,256]{2,1,0:T(8,128)S(1)} %get-tuple-element.16), channel_id=1, source_target_pairs={{0,4},{4,0},{8,12},{12,8},{16,20},{20,16},{24,28},{28,24},{32,36},... | collective-permute-start | bytes 98312 | tf_op jit(solution)/shard_map/ppermute | solution.py:300
  43.0 2.1 %collective-permute-start.4 = (f32[4,8,256]{2,1,0:T(8,128)S(1)}, f32[4,8,256]{2,1,0:T(8,128)S(1)}, u32[]{:S(2)}, u32[]{:S(2)}) collective-permute-start(f32[4,8,256]{2,1,0:T(8,128)S(1)} %get-tuple-element.17), channel_id=1, source_target_pairs={{0,8},{4,12},{8,0},{12,4},{16,24},{20,28},{24,16},{28,20},{32,40},... | collective-permute-start | bytes 98312 | tf_op jit(solution)/shard_map/ppermute | solution.py:300
  45.1 1.2 %collective-permute-start.5 = (f32[4,8,256]{2,1,0:T(8,128)S(1)}, f32[4,8,256]{2,1,0:T(8,128)S(1)}, u32[]{:S(2)}, u32[]{:S(2)}) collective-permute-start(f32[4,8,256]{2,1,0:T(8,128)S(1)} %get-tuple-element.18), channel_id=1, source_target_pairs={{0,12},{4,8},{8,4},{12,0},{16,28},{20,24},{24,20},{28,16},{32,44},... | collective-permute-start | bytes 98312 | tf_op jit(solution)/shard_map/ppermute | solution.py:300
  46.3 0.0 collective-permute-done.3.b_ref
  46.4 1.5 %collective-permute-done.4.c_ref = f32[4,8,256]{2,1,0:T(8,128)S(1)} collective-permute-done((f32[4,8,256]{2,1,0:T(8,128)S(1)}, f32[4,8,256]{2,1,0:T(8,128)S(1)}, u32[]{:S(2)}, u32[]{:S(2)}) %collective-permute-start.4) | collective-permute-done | bytes 32800 | tf_op jit(solution)/shard_map/ppermute | solution.py:300
  47.8 3.0 %collective-permute-done.5.d_ref = f32[4,8,256]{2,1,0:T(8,128)S(1)} collective-permute-done((f32[4,8,256]{2,1,0:T(8,128)S(1)}, f32[4,8,256]{2,1,0:T(8,128)S(1)}, u32[]{:S(2)}, u32[]{:S(2)}) %collective-permute-start.5) | collective-permute-done | bytes 32800 | tf_op jit(solution)/shard_map/ppermute | solution.py:300
  50.8 0.6 %shard_map.76 = f32[8,4,256]{2,1,0:T(4,128)} custom-call(f32[4,8,256]{2,1,0:T(8,128)S(1)} %get-tuple-element.12.scale_ref, f32[4,8,256]{2,1,0:T(8,128)S(1)} %get-tuple-element.15.a_ref, f32[4,8,256]{2,1,0:T(8,128)S(1)} %collective-permute-done.3.b_ref, f32[4,8,256]{2,1,0:T(8,128)S(1)} %collective-permute-done.4.c_ref, ...), custom_call_target="tpu_custom_call" | custom-call | flops 65536 | bytes 262144 | tf_op jit(solution)/shard_map/pallas_call | solution.py:281
  (8 shorter events, 0.1 us)
Async XLA Ops:
  0.0 7.1 %copy-start = (f32[256,512]{1,0:T(8,128)S(1)}, f32[256,512]{1,0:T(8,128)}, u32[]{:S(2)}) copy-start(f32[256,512]{1,0:T(8,128)} %constant.76.clone.right_ref) | copy-start | bytes 1572868
  0.0 7.1 %copy-start.1 = (f32[32,32]{1,0:T(8,128)S(1)}, f32[32,32]{1,0:T(8,128)}, u32[]{:S(2)}) copy-start(f32[32,32]{1,0:T(8,128)} %constant.77.clone.ahead_ref) | copy-start | bytes 12292
  0.0 7.1 %copy-start.2 = (f32[32,32]{1,0:T(8,128)S(1)}, f32[32,32]{1,0:T(8,128)}, u32[]{:S(2)}) copy-start(f32[32,32]{1,0:T(8,128)} %constant.78.clone.back_ref) | copy-start | bytes 12292
  0.0 6.9 %copy-start.4 = (f32[1,16,16,16]{3,2,1,0:T(8,128)S(1)}, f32[1,16,16,16]{3,2,1,0:T(8,128)}, u32[]{:S(2)}) copy-start(f32[1,16,16,16]{3,2,1,0:T(8,128)} %param.8) | copy-start | bytes 49156
  1.3 29.3 %copy-start.3 = (bf16[512,768]{1,0:T(8,128)(2,1)S(1)}, bf16[512,768]{1,0:T(8,128)(2,1)}, u32[]{:S(2)}) copy-start(bf16[512,768]{1,0:T(8,128)(2,1)} %constant.79.clone.spread_ref) | copy-start | bytes 2359300
  1.5 25.3 %collective-permute-start = (f32[32,8,256]{2,1,0:T(8,128)S(1)}, f32[32,8,256]{2,1,0:T(8,128)S(1)}, u32[]{:S(2)}, u32[]{:S(2)}) collective-permute-start(f32[32,8,256]{2,1,0:T(8,128)S(1)} %maximum_bitcast_fusion.own_ref), channel_id=1, source_target_pairs={{0,1},{1,0},{2,3},{3,2},{4,5},{5,4},{6,7},{7,6},{8,9},{9,8},{10,11... | collective-permute-start | bytes 786440 | tf_op jit(solution)/shard_map/ppermute | solution.py:320
  1.6 25.2 %collective-permute-start.1 = (f32[32,8,256]{2,1,0:T(8,128)S(1)}, f32[32,8,256]{2,1,0:T(8,128)S(1)}, u32[]{:S(2)}, u32[]{:S(2)}) collective-permute-start(f32[32,8,256]{2,1,0:T(8,128)S(1)} %maximum_bitcast_fusion.own_ref), channel_id=1, source_target_pairs={{1,2},{2,1},{5,6},{6,5},{9,10},{10,9},{13,14},{14,13},{17,18},{18,... | collective-permute-start | bytes 786440 | tf_op jit(solution)/shard_map/ppermute | solution.py:321
  19.5 11.1 %collective-permute-start.2 = (f32[256,128]{1,0:T(8,128)S(1)}, f32[256,128]{1,0:T(8,128)S(1)}, u32[]{:S(2)}, u32[]{:S(2)}) collective-permute-start(f32[256,128]{1,0:T(8,128)S(1)} %bitcast.10), channel_id=1, source_target_pairs={{0,16},{4,20},{8,24},{12,28},{16,0},{20,4},{24,8},{28,12},{32,48},... | collective-permute-start | bytes 393224 | tf_op jit(solution)/shard_map/ppermute | solution.py:300
  41.9 4.5 %collective-permute-start.3 = (f32[4,8,256]{2,1,0:T(8,128)S(1)}, f32[4,8,256]{2,1,0:T(8,128)S(1)}, u32[]{:S(2)}, u32[]{:S(2)}) collective-permute-start(f32[4,8,256]{2,1,0:T(8,128)S(1)} %get-tuple-element.16), channel_id=1, source_target_pairs={{0,4},{4,0},{8,12},{12,8},{16,20},{20,16},{24,28},{28,24},{32,36},... | collective-permute-start | bytes 98312 | tf_op jit(solution)/shard_map/ppermute | solution.py:300
  43.0 4.8 %collective-permute-start.4 = (f32[4,8,256]{2,1,0:T(8,128)S(1)}, f32[4,8,256]{2,1,0:T(8,128)S(1)}, u32[]{:S(2)}, u32[]{:S(2)}) collective-permute-start(f32[4,8,256]{2,1,0:T(8,128)S(1)} %get-tuple-element.17), channel_id=1, source_target_pairs={{0,8},{4,12},{8,0},{12,4},{16,24},{20,28},{24,16},{28,20},{32,40},... | collective-permute-start | bytes 98312 | tf_op jit(solution)/shard_map/ppermute | solution.py:300
  45.1 5.7 %collective-permute-start.5 = (f32[4,8,256]{2,1,0:T(8,128)S(1)}, f32[4,8,256]{2,1,0:T(8,128)S(1)}, u32[]{:S(2)}, u32[]{:S(2)}) collective-permute-start(f32[4,8,256]{2,1,0:T(8,128)S(1)} %get-tuple-element.18), channel_id=1, source_target_pairs={{0,12},{4,8},{8,4},{12,0},{16,28},{20,24},{24,20},{28,16},{32,44},... | collective-permute-start | bytes 98312 | tf_op jit(solution)/shard_map/ppermute | solution.py:300

commit v3 on v2

--- a/solution.py
+++ b/solution.py
@@ -21,7 +21,7 @@
 KDIM = TS * 48
 EXACT = lax.Precision.HIGHEST
 VMEM = pl.BlockSpec(memory_space=pltpu.VMEM)
-SMEM = pl.BlockSpec(memory_space=pltpu.SMEM)
+HBM = pl.BlockSpec(memory_space=pltpu.HBM)
 
 
 def plus(a, b):
@@ -103,6 +103,11 @@
     return high, (value - high.astype(jnp.float32)).astype(jnp.bfloat16)
 
 
+def two_terms(table):
+    high = np.asarray(table, jnp.bfloat16)
+    return np.stack([high, np.asarray(table - high.astype(np.float64), jnp.bfloat16)])
+
+
 def filter_tables():
     small = np.arange(TS)
     pair = 2.0 * math.pi * np.outer(small, small) / TS
@@ -112,37 +117,81 @@
     c, s = np.cos(pair), np.sin(pair)
     ahead = np.block([[c, s], [-s, c]])
     back = np.block([[c, -s], [s, c]])
-    return tuple(np.asarray(t, np.float32) for t in (right, ahead, back))
+    return two_terms(right), np.float32(np.stack([ahead, back]))
 
 
 def spread_table():
-    out = np.zeros((2, TS, TS, TS, 48), np.float32)
-    for part in range(2):
-        for b in range(TS):
-            for c in range(TS):
-                out[part, b, c, b, 24 * part + c] = 1.0
-    return out.reshape(2 * TS * TS, KDIM)
-
-
-def filter_kernel(template_ref, wedge_ref, right_ref, ahead_ref, back_ref, out_ref):
-    def product(a, b):
+    out = np.zeros((TS, TS, TS, 24), np.float32)
+    for b in range(TS):
+        for c in range(TS):
+            out[c, b, b, c] = 1.0
+    return out.reshape(TS * TS, KDIM // 2)
+
+
+def front_kernel(
+    template_hbm, wedge_hbm, right_hbm, small_hbm, out_ref,
+    template_ref, wedge_ref, right_ref, small_ref, sems,
+):
+    width = TS * TS
+    copies = [
+        pltpu.make_async_copy(src, dst, sems.at[i])
+        for i, (src, dst) in enumerate(
+            ((template_hbm, template_ref), (right_hbm, right_ref), (small_hbm, small_ref), (wedge_hbm, wedge_ref))
+        )
+    ]
+    for copy in copies:
+        copy.start()
+
+    def flat(ref):
+        return jnp.concatenate([ref[c].astype(jnp.float32) for c in range(TS)], axis=1)
+
+    def exact(a, b):
         return jnp.dot(a, b, precision=EXACT, preferred_element_type=jnp.float32)
 
-    width = TS * TS
-    spec = product(template_ref[...], right_ref[...])
+    def product(value, lanes):
+        rows = value.shape[0]
+        both = jnp.concatenate(halves(value), axis=0)
+        out = jnp.dot(both, right_ref[0, :, lanes], preferred_element_type=jnp.float32)
+        low = jnp.dot(both[:rows], right_ref[1, :, lanes], preferred_element_type=jnp.float32)
+        return out[:rows] + (out[rows:] + low)
+
+    for copy in copies:
+        copy.wait()
+    spec = product(flat(template_ref), slice(0, 2 * width))
     spec = jnp.concatenate([spec[:, :width], spec[:, width:]], axis=0)
-    keep = wedge_ref[...]
-    spec = product(ahead_ref[...], spec) * jnp.concatenate([keep, keep], axis=0)
-    spec = product(back_ref[...], spec)
-    filt = product(spec[:TS], right_ref[:, :width]) + product(spec[TS:], right_ref[:, width:])
+    keep = flat(wedge_ref)
+    spec = exact(small_ref[0], spec) * jnp.concatenate([keep, keep], axis=0)
+    spec = exact(small_ref[1], spec)
+    filt = product(spec[:TS], slice(0, width)) + product(spec[TS:], slice(width, 2 * width))
     filt = filt * (1.0 / float(TS**3))
     centered = filt - jnp.sum(filt) * (1.0 / float(TS**3))
-    normed = centered / jnp.sqrt(jnp.sum(centered * centered) + 1e-05)
-    out_ref[...] = jnp.concatenate([normed[:, :LANES], normed[:, LANES:]], axis=0)
-
-
-def volume_kernel(place_ref, inside_ref, own_ref, across_ref, high_ref, low_ref, scale_ref, spec_ref):
-    even = place_ref[1] % 2 == 0
+    out_ref[...] = centered / jnp.sqrt(jnp.sum(centered * centered) + 1e-05)
+
+
+def window_kernel(after_ref, volume_hbm, window_ref, piece_ref, sems):
+    rows = volume_hbm.shape[1]
+    first = lax.axis_index("orient") // GROUP * 16 + (rows - HALF)
+    pieces = []
+    for j in range(NF // 8):
+        at = pl.multiple_of(lax.rem(first + 8 * j, rows), 8)
+        for h in range(NY // LANES):
+            copy = pltpu.make_async_copy(
+                volume_hbm.at[:, pl.ds(at, 8), pl.ds(h * LANES, LANES)],
+                piece_ref.at[h, :, pl.ds(8 * j, 8), :],
+                sems.at[len(pieces)],
+            )
+            copy.start()
+            pieces.append(copy)
+    for copy in pieces:
+        copy.wait()
+    flat_piece = piece_ref.reshape(NY // LANES, SLAB * NF, LANES)
+    for h in range(NY // LANES):
+        for x in range(NF):
+            window_ref[x, :, h * LANES : (h + 1) * LANES] = flat_piece[h, pl.ds(x, SLAB, stride=NF), :]
+
+
+def volume_kernel(inside_ref, own_ref, across_ref, high_ref, low_ref, spec_ref):
+    even = lax.rem(lax.axis_index("zslab"), 2) == 0
     inside_at = pl.multiple_of(jnp.where(even, 16, 0), 8)
     across_at = pl.multiple_of(16 - inside_at, 8)
     for ref, start in ((inside_ref, inside_at), (own_ref, 8), (across_ref, across_at)):
@@ -153,11 +202,21 @@
                 spec_ref[k, pl.ds(start + 24, 8), lane : lane + LANES] = im
 
     def split(k, carry):
-        high_ref[k], low_ref[k] = halves(spec_ref[k])
+        nil = jnp.zeros((8, NY), jnp.float32)
+        for part in range(2):
+            a, b, c = (spec_ref[k, 24 * part + 8 * j : 24 * part + 8 * j + 8, :] for j in range(3))
+            rows = slice(64 * part, 64 * part + 64)
+            high_ref[k, rows], low_ref[k, rows] = halves(
+                jnp.concatenate([a, b, c, nil, nil, a, b, c], axis=0)
+            )
         return carry
 
     lax.fori_loop(0, NK, split, 0)
-    first = place_ref[0] * STRIP
+
+
+def scale_kernel(inside_ref, own_ref, across_ref, scale_ref):
+    even = lax.rem(lax.axis_index("zslab"), 2) == 0
+    first = lax.rem(lax.axis_index("orient"), GROUP) * STRIP
     sums = []
     for x in range(STRIP + TS - 1):
         inside, across = inside_ref[first + x], across_ref[first + x]
@@ -179,50 +238,59 @@
 
 
 def score_kernel(
-    place_ref, a_ref, b_ref, spread_ref, high_ref, low_ref,
+    gathered_ref, spread_ref, high_ref, low_ref,
     out0_ref, out1_ref, out2_ref, out3_ref,
-    spec_ref, base_ref, left_a, left_b, high_a, high_b, low_a, low_b, prod_ref, best_ref,
+    wide_ref, base_ref, left_a, left_b, high_a, high_b, low_a, low_b, prod_ref, best_ref,
 ):
-    width = TS * TS
-    for lane in range(0, width, LANES):
-        start = lane // LANES * TS
+    side = KDIM // 2
+    high, low = halves(gathered_ref[...])
+    wide = jnp.dot(high, spread_ref[...], preferred_element_type=jnp.float32) + jnp.dot(
+        low, spread_ref[...], preferred_element_type=jnp.float32
+    )
+    for j in range(side // LANES):
+        wide_ref[j] = wide[:, j * LANES : (j + 1) * LANES]
+    for j in range(side // LANES):
         groups = []
-        for ref in (a_ref, b_ref):
-            rows = [ref[pl.ds(start + a, 8, stride=2 * TS), :] for a in range(TS)]
+        for o in (0, 8):
+            rows = [wide_ref[j, pl.ds(o * TS + a, 8, stride=TS), :] for a in range(TS)]
             groups.append(slots(forward(rows + [None] * (NF - TS))))
         for k, ((re0, im0), (re1, im1)) in enumerate(zip(*groups)):
             re = halves(jnp.concatenate([re0, re1], axis=0))
             im = halves(jnp.concatenate([im0, im1], axis=0))
             for h in range(2):
-                row, nil = 64 * k + 32 * h, jnp.zeros_like(re[h])
-                left, right = slice(lane, lane + LANES), slice(width + lane, width + lane + LANES)
-                spec_ref[row : row + NO, left] = re[h]
-                spec_ref[row : row + NO, right] = nil if k == 0 else im[h]
-                spec_ref[row + NO : row + 2 * NO, left] = nil if k == 0 else -im[h]
-                spec_ref[row + NO : row + 2 * NO, right] = im[h] if k == 0 else re[h]
-
-    def expand(i, carry):
-        row = pl.multiple_of(i * 256, 256)
-        base_ref[pl.ds(row, 256), :] = jnp.dot(
-            spec_ref[pl.ds(row, 256), :], spread_ref[...], preferred_element_type=jnp.float32
-        ).astype(jnp.bfloat16)
-        return carry
-
-    lax.fori_loop(0, 4, expand, 0)
+                base_ref[k, h, 0, :, j * LANES : (j + 1) * LANES] = re[h]
+                base_ref[k, h, 1, :, j * LANES : (j + 1) * LANES] = im[h]
+
+    def turned(value, shift, axis=1):
+        shift = shift % value.shape[axis]
+        return value if shift == 0 else pltpu.roll(value, shift, axis=axis)
 
     def build(k, left, right_high, right_low):
         for h in range(2):
+            re, im = base_ref[k, h, 0], base_ref[k, h, 1]
+            for z in range(SLAB):
+                row = h * 256 + z * NO
+                rows, more = slice(row, row + NO), slice(row + 128, row + 128 + NO)
+                re_z, im_z = turned(re, z), turned(im, z)
+                left[rows, :side] = re_z
+                if isinstance(k, int) and k == 0:
+                    nil = jnp.zeros_like(re_z)
+                    left[rows, side:] = nil
+                    left[more, :side] = nil
+                    left[more, side:] = im_z
+                else:
+                    left[rows, side:] = im_z
+                    left[more, :side] = -im_z
+                    left[more, side:] = re_z
+        for src, dst in ((high_ref, right_high), (low_ref, right_low)):
             for part in range(2):
-                at = pl.multiple_of(k * 64 + 32 * h + 16 * part, 16)
-                value = base_ref[pl.ds(at, NO), :]
-                for z in range(SLAB):
-                    row = h * 256 + part * 128 + z * NO
-                    left[row : row + NO, :] = value if z == 0 else pltpu.roll(value, z, axis=1)
-        for src, dst in ((high_ref, right_high), (low_ref, right_low)):
-            value = src[k]
-            for b in range(TS):
-                shift = (HALF - b) % NY
-                dst[48 * b : 48 * b + 48, :] = value if shift == 0 else pltpu.roll(value, shift, axis=1)
+                a, b, c, d = (src[k, 64 * part + 16 * j : 64 * part + 16 * j + 16, :] for j in range(4))
+                for y in range(0, TS, 2):
+                    row = side * part + 24 * y
+                    here, after = HALF - y, HALF - y - 1
+                    dst[row : row + 16, :] = turned(a, here)
+                    dst[row + 16 : row + 32, :] = turned(b, here) + turned(c, after)
+                    dst[row + 32 : row + 48, :] = turned(d, after)
 
     def multiply(k, left, right_high, right_low):
         both = jnp.dot(left[...], right_high[...], preferred_element_type=jnp.float32)
@@ -266,7 +334,7 @@
         return carry
 
     lax.fori_loop(0, SLAB, finish, 0)
-    mine = place_ref[0]
+    mine = lax.rem(lax.axis_index("orient"), GROUP)
     for m, ref in enumerate((out0_ref, out1_ref, out2_ref, out3_ref)):
         ref[...] = best_ref[pl.ds((mine ^ m) * STRIP, STRIP)]
 
@@ -277,14 +345,14 @@
         out_ref[:, x, :] = top * scale_ref[x]
 
 
-def call(kernel, outs, scratch, args, specs, flops=0, nbytes=0):
+def call(kernel, outs, scratch, args, specs, flops=0, nbytes=0, limit=48 * 1024 * 1024):
     return pl.pallas_call(
         kernel,
         out_shape=outs,
         in_specs=specs,
         out_specs=[VMEM] * len(outs) if isinstance(outs, (list, tuple)) else VMEM,
         scratch_shapes=scratch,
-        compiler_params=pltpu.CompilerParams(vmem_limit_bytes=48 * 1024 * 1024),
+        compiler_params=pltpu.CompilerParams(vmem_limit_bytes=limit),
         cost_estimate=pl.CostEstimate(flops=flops, bytes_accessed=nbytes, transcendentals=0),
     )(*args)
 
@@ -292,50 +360,49 @@
 def shards(volume, templates, wedge):
     f32, bf16 = jnp.float32, jnp.bfloat16
     count = lax.axis_size("orient")
-    me = lax.axis_index("orient")
-    place = jnp.stack([me % GROUP, lax.axis_index("zslab")]).astype(jnp.int32)
-    region = me // GROUP
-
     def swap(value, mask):
         return lax.ppermute(value, "orient", [(i, i ^ mask) for i in range(count)])
 
-    template = jnp.transpose(templates[0], (1, 2, 0)).reshape(TS, TS * TS)
-    keep = jnp.transpose(wedge.astype(f32), (1, 2, 0)).reshape(TS, TS * TS)
+    right, small = (jnp.asarray(t) for t in filter_tables())
     normed = call(
-        filter_kernel, jax.ShapeDtypeStruct((2 * TS, LANES), f32), [],
-        (template, keep) + filter_tables(), [VMEM] * 5, 1 << 22, 1 << 20,
-    )
+        front_kernel, pltpu.VMEM((TS, TS * TS), f32),
+        [
+            pltpu.VMEM((TS, TS, TS), f32),
+            pltpu.VMEM((TS, TS, TS), jnp.int32),
+            pltpu.VMEM(right.shape, bf16),
+            pltpu.VMEM(small.shape, f32),
+            pltpu.SemaphoreType.DMA((4,)),
+        ],
+        (templates[0], wedge, right, small), [HBM] * 4, 1 << 22, 1 << 20, None,
+    )
+    other = swap(normed, 4)
+    window = call(
+        window_kernel, pltpu.VMEM((NF, SLAB, NY), f32),
+        [pltpu.VMEM((NY // LANES, SLAB, NF, LANES), f32), pltpu.SemaphoreType.DMA((8,))],
+        (normed, volume), [VMEM, HBM], 0, 1 << 19, None,
+    )
+    fan = jnp.broadcast_to(jnp.concatenate([normed, other], axis=0), (8, 2 * TS, TS * TS))
     near = [[8 * a + b for a in range(8)] for b in range(8)]
-    eight = lax.all_to_all(
-        jnp.broadcast_to(normed, (8, 2 * TS, LANES)), "orient", 0, 0, tiled=True, axis_index_groups=near
-    ).reshape(16 * TS, LANES)
-    gathered = [eight, swap(eight, 4)]
-
-    rows = volume.shape[1]
-    pieces = [
-        lax.dynamic_slice_in_dim(volume, (region * 16 - HALF + 8 * j) % rows, 8, 1) for j in range(4)
-    ]
-    window = jnp.transpose(jnp.concatenate(pieces, axis=1), (1, 0, 2))
+    gathered = lax.all_to_all(
+        fan, "orient", 0, 0, tiled=True, axis_index_groups=near
+    ).reshape(NO * TS, TS * TS)
+
     slabs = lax.axis_size("zslab")
     inside = lax.ppermute(window, "zslab", [(s, s ^ 1) for s in range(slabs)])
     across = lax.ppermute(window, "zslab", [(1, 2), (2, 1)])
-    high, low, scale = call(
-        volume_kernel,
-        (
-            jax.ShapeDtypeStruct((NK, 48, NY), bf16),
-            jax.ShapeDtypeStruct((NK, 48, NY), bf16),
-            jax.ShapeDtypeStruct((STRIP, SLAB, NY), f32),
-        ),
-        [pltpu.VMEM((NK, 48, NY), f32)],
-        (place, inside, window, across), [SMEM] + [VMEM] * 3, 1 << 24, 1 << 21,
+    inside, gathered = lax.optimization_barrier((inside, gathered))
+    spectrum = jax.ShapeDtypeStruct((NK, 128, NY), bf16)
+    high, low = call(
+        volume_kernel, (spectrum, spectrum), [pltpu.VMEM((NK, 48, NY), f32)],
+        (inside, window, across), [VMEM] * 3, 1 << 24, 1 << 21,
     )
     spread = jnp.asarray(spread_table(), bf16)
     strip = jax.ShapeDtypeStruct((STRIP, SLAB, NY), f32)
     parts = call(
         score_kernel, (strip,) * 4,
         [
-            pltpu.VMEM((NK * 64, 2 * TS * TS), bf16),
-            pltpu.VMEM((NK * 64, KDIM), bf16),
+            pltpu.VMEM((KDIM // 2 // LANES, NO * TS, LANES), f32),
+            pltpu.VMEM((NK, 2, 2, NO, KDIM // 2), bf16),
             pltpu.VMEM((512, KDIM), bf16),
             pltpu.VMEM((512, KDIM), bf16),
             pltpu.VMEM((KDIM, NY), bf16),
@@ -345,7 +412,11 @@
             pltpu.VMEM((NK, 256, NY), f32),
             pltpu.VMEM((NF // 2, SLAB, NY), f32),
         ],
-        (place, *gathered, spread, high, low), [SMEM] + [VMEM] * 5, 1 << 33, 1 << 21,
+        (gathered, spread, high, low), [VMEM] * 4, 1 << 33, 1 << 21,
+    )
+    late, _ = lax.optimization_barrier((inside, parts[1]))
+    scale = call(
+        scale_kernel, strip, [], (late, window, across), [VMEM] * 3, 1 << 22, 1 << 20
     )
     arrived = [parts[0]] + [swap(parts[m], m) for m in range(1, GROUP)]
     return call(

time: 51.7 us -> 46.7 us (0.903)
  the two profiles are of different devices: /device:TPU:4 before, /device:TPU:2 now
where the time goes in v3:
time: 46.7 us; the launch traced here: 46.3 us
  Pallas kernels  15.1 us (32%)
  starting transfers between devices  15.1 us (32%)
  blocking collectives  11.7 us (25%)
  waiting for transfers between devices  3.59 us (8%)
  other arithmetic  0.72 us (2%)
    pallas_call x6, Pallas kernels, call(): pl.pallas_call(kernel, out_shape=outs, in_specs=specs, out_specs=[VMEM] *...  15.1 us
    all_to_all x1, blocking collectives, shards(): lax.all_to_all(fan, 'orient', 0, 0, tiled=True, axis_index_groups=near)  11.7 us
    ppermute x4, starting transfers between devices, swap(): return lax.ppermute(value, 'orient', [(i, i ^ mask) for i in range(count)])  10.9 us
    ppermute x4, waiting for transfers between devices, swap(): return lax.ppermute(value, 'orient', [(i, i ^ mask) for i in range(count)])  3.59 us
    ppermute x1, starting transfers between devices, shards(): inside = lax.ppermute(window, 'zslab', [(s, s ^ 1) for s in range(slabs)])  3.56 us
  transfers between devices with their start and end apart: 6, of which 3 were waited for; matrix products, arithmetic and copies ran while one was open for 2% of the time, Pallas kernels for 5%

profile of v3, /device:TPU:2, one launch (start us, length us, event | category | flops | bytes accessed | tf_op | source)
XLA Modules:
  0.0 46.3 jit_solution(17352009735369710952)
XLA Ops:
  0.0 2.3 %shard_map.64.after_ref = f32[16,256]{1,0:T(8,128)S(1)} custom-call(f32[16,16,16]{2,1,0:T(8,128)} %bitcast.3, s32[16,16,16]{2,1,0:T(8,128)} %wedge_hbm.1, bf16[2,256,512]{2,1,0:T(8,128)(2,1)} %constant.6.clone.right_hbm, f32[2,32,32]{2,1,0:T(8,128)} %constant.7.clone.small_hbm), custom_call_target="tpu_custom_call" | custom-call | flops 4194304 | bytes 1048576 | tf_op jit(solution)/shard_map/pallas_call | solution.py:349
  2.3 0.0 copy-start
  2.3 0.0 copy-start.1
  2.3 7.3 %collective-permute-start.1 = (f32[16,256]{1,0:T(8,128)S(1)}, f32[16,256]{1,0:T(8,128)S(1)}, u32[]{:S(2)}, u32[]{:S(2)}) collective-permute-start(f32[16,256]{1,0:T(8,128)S(1)} %shard_map.64.after_ref), channel_id=1, source_target_pairs={{0,16},{4,20},{8,24},{12,28},{16,0},{20,4},{24,8},{28,12},{32,48},... | collective-permute-start | bytes 49160 | tf_op jit(solution)/shard_map/ppermute | solution.py:364
  9.6 0.0 copy-done
  9.6 1.8 %shard_map.65.own_ref = f32[32,8,256]{2,1,0:T(8,128)S(1)} custom-call(f32[16,256]{1,0:T(8,128)} %copy-done, f32[8,256,256]{2,1,0:T(8,128)} %volume_hbm.1), custom_call_target="tpu_custom_call" | custom-call | bytes 524288 | tf_op jit(solution)/shard_map/pallas_call | solution.py:349
  11.4 0.7 %collective-permute-start.2 = (f32[32,8,256]{2,1,0:T(8,128)S(1)}, f32[32,8,256]{2,1,0:T(8,128)S(1)}, u32[]{:S(2)}, u32[]{:S(2)}) collective-permute-start(f32[32,8,256]{2,1,0:T(8,128)S(1)} %shard_map.65.own_ref), channel_id=1, source_target_pairs={{1,2},{2,1},{5,6},{6,5},{9,10},{10,9},{13,14},{14,13},{17,18},{18,... | collective-permute-start | bytes 786440 | tf_op jit(solution)/shard_map/ppermute | solution.py:392
  12.1 3.6 %collective-permute-start = (f32[32,8,256]{2,1,0:T(8,128)S(1)}, f32[32,8,256]{2,1,0:T(8,128)S(1)}, u32[]{:S(2)}, u32[]{:S(2)}) collective-permute-start(f32[32,8,256]{2,1,0:T(8,128)S(1)} %shard_map.65.own_ref), channel_id=1, source_target_pairs={{0,1},{1,0},{2,3},{3,2},{4,5},{5,4},{6,7},{7,6},{8,9},{9,8},{10,11... | collective-permute-start | bytes 786440 | tf_op jit(solution)/shard_map/ppermute | solution.py:391
  15.6 0.0 collective-permute-done.1
  15.6 0.7 %pad_maximum_fusion = f32[32,256]{1,0:T(8,128)S(1)} fusion(f32[16,256]{1,0:T(8,128)S(1)} %collective-permute-done.1, f32[16,256]{1,0:T(8,128)} %copy-done), kind=kLoop, calls=%fused_computation | loop fusion | flops 8192 | bytes 65536 | tf_op jit(solution)/shard_map/concatenate | solution.py:384
  16.4 11.7 %all_to_all.5 = f32[8,32,256]{2,1,0:T(8,128)S(1)} all-to-all(f32[8,32,256]{2,1,0:T(8,128)S(1)} %broadcast_in_dim.3), channel_id=1, replica_groups={{0,32,64,96,128,160,192,224},{4,36,68,100,132,164,196,228},{8,40,72,104..., dimensions={0} | all-to-all | bytes 524288 | tf_op jit(solution)/shard_map/all_to_all | solution.py:386
  28.1 0.0 collective-permute-done.inside_ref
  28.1 0.0 collective-permute-done.2.across_ref
  28.1 0.5 %shard_map.66 = (bf16[16,128,256]{2,1,0:T(8,128)(2,1)S(1)}, bf16[16,128,256]{2,1,0:T(8,128)(2,1)S(1)}) custom-call(f32[32,8,256]{2,1,0:T(8,128)S(1)} %collective-permute-done.inside_ref, f32[32,8,256]{2,1,0:T(8,128)S(1)} %shard_map.65.own_ref, f32[32,8,256]{2,1,0:T(8,128)S(1)} %collective-permute-done.2.across_ref), custom_call_target="tpu_custom_call" | custom-call | flops 16777216 | bytes 2097152 | tf_op jit(solution)/shard_map/pallas_call | solution.py:349
  28.6 0.0 copy-done.1
  28.6 9.4 %shard_map.67 = (f32[4,8,256]{2,1,0:T(8,128)S(1)}, f32[4,8,256]{2,1,0:T(8,128)S(1)}, f32[4,8,256]{2,1,0:T(8,128)S(1)}, f32[4,8,256]{2,1,0:T(8,128)S(1)}) custom-call(f32[256,256]{1,0:T(8,128)S(1)} %bitcast.2, bf16[256,384]{1,0:T(8,128)(2,1)S(1)} %copy-done.1, bf16[16,128,256]{2,1,0:T(8,128)(2,1)S(1)} %get-tuple-element.16.high_ref, ...), custom_call_target="tpu_custom_call" | custom-call | flops 8589934592 | bytes 2097152 | tf_op jit(solution)/shard_map/pallas_call | solution.py:349
  38.1 1.6 %collective-permute-start.4 = (f32[4,8,256]{2,1,0:T(8,128)S(1)}, f32[4,8,256]{2,1,0:T(8,128)S(1)}, u32[]{:S(2)}, u32[]{:S(2)}) collective-permute-start(f32[4,8,256]{2,1,0:T(8,128)S(1)} %get-tuple-element.21), channel_id=1, source_target_pairs={{0,8},{4,12},{8,0},{12,4},{16,24},{20,28},{24,16},{28,20},{32,40},... | collective-permute-start | bytes 98312 | tf_op jit(solution)/shard_map/ppermute | solution.py:364
  39.6 1.9 %collective-permute-start.5 = (f32[4,8,256]{2,1,0:T(8,128)S(1)}, f32[4,8,256]{2,1,0:T(8,128)S(1)}, u32[]{:S(2)}, u32[]{:S(2)}) collective-permute-start(f32[4,8,256]{2,1,0:T(8,128)S(1)} %get-tuple-element.22), channel_id=1, source_target_pairs={{0,12},{4,8},{8,4},{12,0},{16,28},{20,24},{24,20},{28,16},{32,44},... | collective-permute-start | bytes 98312 | tf_op jit(solution)/shard_map/ppermute | solution.py:364
  41.5 0.1 collective-permute-start.3
  41.6 0.5 shard_map.68.scale_ref
  42.1 0.9 %collective-permute-done.4.c_ref = f32[4,8,256]{2,1,0:T(8,128)S(1)} collective-permute-done((f32[4,8,256]{2,1,0:T(8,128)S(1)}, f32[4,8,256]{2,1,0:T(8,128)S(1)}, u32[]{:S(2)}, u32[]{:S(2)}) %collective-permute-start.4) | collective-permute-done | bytes 32800 | tf_op jit(solution)/shard_map/ppermute | solution.py:364
  43.0 2.3 %collective-permute-done.5.d_ref = f32[4,8,256]{2,1,0:T(8,128)S(1)} collective-permute-done((f32[4,8,256]{2,1,0:T(8,128)S(1)}, f32[4,8,256]{2,1,0:T(8,128)S(1)}, u32[]{:S(2)}, u32[]{:S(2)}) %collective-permute-start.5) | collective-permute-done | bytes 32800 | tf_op jit(solution)/shard_map/ppermute | solution.py:364
  45.4 0.3 collective-permute-done.3.b_ref
  45.7 0.6 %shard_map.69 = f32[8,4,256]{2,1,0:T(4,128)} custom-call(f32[4,8,256]{2,1,0:T(8,128)S(1)} %shard_map.68.scale_ref, f32[4,8,256]{2,1,0:T(8,128)S(1)} %get-tuple-element.20.a_ref, f32[4,8,256]{2,1,0:T(8,128)S(1)} %collective-permute-done.3.b_ref, f32[4,8,256]{2,1,0:T(8,128)S(1)} %collective-permute-done.4.c_ref, f32[4,8,256]{2,1,0:T(8,128)S(1)} %collective-permute-done.5.d_ref), custom_call_target="tpu_custom_call" | custom-call | flops 65536 | bytes 262144 | tf_op jit(solution)/shard_map/pallas_call | solution.py:349
  (1 shorter events, 0.0 us)
Async XLA Ops:
  2.3 7.3 %copy-start = (f32[16,256]{1,0:T(8,128)}, f32[16,256]{1,0:T(8,128)S(1)}, u32[]{:S(2)}) copy-start(f32[16,256]{1,0:T(8,128)S(1)} %shard_map.64.after_ref) | copy-start | bytes 49156
  2.3 26.3 %copy-start.1 = (bf16[256,384]{1,0:T(8,128)(2,1)S(1)}, bf16[256,384]{1,0:T(8,128)(2,1)}, u32[]{:S(2)}) copy-start(bf16[256,384]{1,0:T(8,128)(2,1)} %constant.8.clone.spread_ref) | copy-start | bytes 589828
  2.3 13.3 %collective-permute-start.1 = (f32[16,256]{1,0:T(8,128)S(1)}, f32[16,256]{1,0:T(8,128)S(1)}, u32[]{:S(2)}, u32[]{:S(2)}) collective-permute-start(f32[16,256]{1,0:T(8,128)S(1)} %shard_map.64.after_ref), channel_id=1, source_target_pairs={{0,16},{4,20},{8,24},{12,28},{16,0},{20,4},{24,8},{28,12},{32,48},... | collective-permute-start | bytes 49160 | tf_op jit(solution)/shard_map/ppermute | solution.py:364
  11.4 16.7 %collective-permute-start.2 = (f32[32,8,256]{2,1,0:T(8,128)S(1)}, f32[32,8,256]{2,1,0:T(8,128)S(1)}, u32[]{:S(2)}, u32[]{:S(2)}) collective-permute-start(f32[32,8,256]{2,1,0:T(8,128)S(1)} %shard_map.65.own_ref), channel_id=1, source_target_pairs={{1,2},{2,1},{5,6},{6,5},{9,10},{10,9},{13,14},{14,13},{17,18},{18,... | collective-permute-start | bytes 786440 | tf_op jit(solution)/shard_map/ppermute | solution.py:392
  12.1 16.0 %collective-permute-start = (f32[32,8,256]{2,1,0:T(8,128)S(1)}, f32[32,8,256]{2,1,0:T(8,128)S(1)}, u32[]{:S(2)}, u32[]{:S(2)}) collective-permute-start(f32[32,8,256]{2,1,0:T(8,128)S(1)} %shard_map.65.own_ref), channel_id=1, source_target_pairs={{0,1},{1,0},{2,3},{3,2},{4,5},{5,4},{6,7},{7,6},{8,9},{9,8},{10,11... | collective-permute-start | bytes 786440 | tf_op jit(solution)/shard_map/ppermute | solution.py:391
  38.1 4.9 %collective-permute-start.4 = (f32[4,8,256]{2,1,0:T(8,128)S(1)}, f32[4,8,256]{2,1,0:T(8,128)S(1)}, u32[]{:S(2)}, u32[]{:S(2)}) collective-permute-start(f32[4,8,256]{2,1,0:T(8,128)S(1)} %get-tuple-element.21), channel_id=1, source_target_pairs={{0,8},{4,12},{8,0},{12,4},{16,24},{20,28},{24,16},{28,20},{32,40},... | collective-permute-start | bytes 98312 | tf_op jit(solution)/shard_map/ppermute | solution.py:364
  39.6 5.7 %collective-permute-start.5 = (f32[4,8,256]{2,1,0:T(8,128)S(1)}, f32[4,8,256]{2,1,0:T(8,128)S(1)}, u32[]{:S(2)}, u32[]{:S(2)}) collective-permute-start(f32[4,8,256]{2,1,0:T(8,128)S(1)} %get-tuple-element.22), channel_id=1, source_target_pairs={{0,12},{4,8},{8,4},{12,0},{16,28},{20,24},{24,20},{28,16},{32,44},... | collective-permute-start | bytes 98312 | tf_op jit(solution)/shard_map/ppermute | solution.py:364
  41.5 4.2 %collective-permute-start.3 = (f32[4,8,256]{2,1,0:T(8,128)S(1)}, f32[4,8,256]{2,1,0:T(8,128)S(1)}, u32[]{:S(2)}, u32[]{:S(2)}) collective-permute-start(f32[4,8,256]{2,1,0:T(8,128)S(1)} %get-tuple-element.18), channel_id=1, source_target_pairs={{0,4},{4,0},{8,12},{12,8},{16,20},{20,16},{24,28},{28,24},{32,36},... | collective-permute-start | bytes 98312 | tf_op jit(solution)/shard_map/ppermute | solution.py:364

commit v4 on v3

--- a/solution.py
+++ b/solution.py
@@ -66,27 +66,32 @@
     return bins
 
 
+def inverse_step(bins, count):
+    even, odd = {}, {}
+    for k in range(count // 4 + 1):
+        if k not in bins:
+            continue
+        a, b = bins[k], bins[count // 2 - k]
+        if k == 0:
+            even[k] = (a[0] + b[0], None)
+            odd[k] = (a[0] - b[0], None)
+        elif 4 * k == count:
+            even[k] = (2.0 * a[0], None)
+            odd[k] = (-2.0 * a[1], None)
+        else:
+            even[k] = (a[0] + b[0], a[1] - b[1])
+            odd[k] = twiddled((a[0] - b[0], a[1] + b[1]), k, count, 1.0)
+    return even, odd
+
+
 def inverse(bins, count, need):
     if count == 2:
         first = bins[0][0] + bins[1][0]
         return [first] if need == 1 else [first, bins[0][0] - bins[1][0]]
-    even, odd = [], []
-    for k in range(count // 4 + 1):
-        a, b = bins[k], bins[count // 2 - k]
-        if k == 0:
-            even.append((a[0] + b[0], None))
-            odd.append((a[0] - b[0], None))
-        elif 4 * k == count:
-            even.append((2.0 * a[0], None))
-            odd.append((-2.0 * a[1], None))
-        else:
-            even.append((a[0] + b[0], a[1] - b[1]))
-            odd.append(twiddled((a[0] - b[0], a[1] + b[1]), k, count, 1.0))
-    evens = inverse(even, count // 2, (need + 1) // 2)
-    odds = inverse(odd, count // 2, need // 2)
+    even, odd = inverse_step(bins, count)
     rows = [None] * need
-    rows[::2] = evens
-    rows[1::2] = odds
+    rows[::2] = inverse(even, count // 2, (need + 1) // 2)
+    rows[1::2] = inverse(odd, count // 2, need // 2)
     return rows
 
 
@@ -94,8 +99,7 @@
     return [(bins[0][0], bins[NK][0])] + [bins[k] for k in range(1, NK)]
 
 
-def unslot(pairs):
-    return [(pairs[0][0], None)] + list(pairs[1:]) + [(pairs[0][1], None)]
+QUADS = ((0, 4, 8, 12), (1, 7, 9, 15), (2, 6, 10, 14), (3, 5, 11, 13))
 
 
 def halves(value):
@@ -129,7 +133,7 @@
 
 
 def front_kernel(
-    template_hbm, wedge_hbm, right_hbm, small_hbm, out_ref,
+    template_hbm, wedge_hbm, right_hbm, small_hbm, out_ref, token_ref,
     template_ref, wedge_ref, right_ref, small_ref, sems,
 ):
     width = TS * TS
@@ -166,6 +170,7 @@
     filt = filt * (1.0 / float(TS**3))
     centered = filt - jnp.sum(filt) * (1.0 / float(TS**3))
     out_ref[...] = centered / jnp.sqrt(jnp.sum(centered * centered) + 1e-05)
+    token_ref[...] = jnp.zeros_like(token_ref)
 
 
 def window_kernel(after_ref, volume_hbm, window_ref, piece_ref, sems):
@@ -188,6 +193,12 @@
     for h in range(NY // LANES):
         for x in range(NF):
             window_ref[x, :, h * LANES : (h + 1) * LANES] = flat_piece[h, pl.ds(x, SLAB, stride=NF), :]
+
+
+def fan_kernel(own_ref, other_ref, out_ref):
+    own, other = own_ref[...], other_ref[...]
+    for i in range(out_ref.shape[0]):
+        out_ref[i, :TS], out_ref[i, TS:] = own, other
 
 
 def volume_kernel(inside_ref, own_ref, across_ref, high_ref, low_ref, spec_ref):
@@ -240,7 +251,7 @@
 def score_kernel(
     gathered_ref, spread_ref, high_ref, low_ref,
     out0_ref, out1_ref, out2_ref, out3_ref,
-    wide_ref, base_ref, left_a, left_b, high_a, high_b, low_a, low_b, prod_ref, best_ref,
+    wide_ref, base_ref, left_a, left_b, high_a, high_b, low_a, low_b, prod_a, prod_b, part_ref, best_ref,
 ):
     side = KDIM // 2
     high, low = halves(gathered_ref[...])
@@ -273,7 +284,7 @@
                 rows, more = slice(row, row + NO), slice(row + 128, row + 128 + NO)
                 re_z, im_z = turned(re, z), turned(im, z)
                 left[rows, :side] = re_z
-                if isinstance(k, int) and k == 0:
+                if k == 0:
                     nil = jnp.zeros_like(re_z)
                     left[rows, side:] = nil
                     left[more, :side] = nil
@@ -292,45 +303,61 @@
                     dst[row + 16 : row + 32, :] = turned(b, here) + turned(c, after)
                     dst[row + 32 : row + 48, :] = turned(d, after)
 
-    def multiply(k, left, right_high, right_low):
+    def multiply(prod, left, right_high, right_low):
         both = jnp.dot(left[...], right_high[...], preferred_element_type=jnp.float32)
         low = jnp.dot(left[:256], right_low[...], preferred_element_type=jnp.float32)
-        prod_ref[k] = both[:256] + (both[256:] + low)
-
-    first, second = (left_a, high_a, low_a), (left_b, high_b, low_b)
-    build(0, *first)
-
-    def two(i, carry):
-        k = 2 * i
-        multiply(k, *first)
-        build(k + 1, *second)
-        multiply(k + 1, *second)
-        build(jnp.minimum(k + 2, NK - 1), *first)
-        return carry
-
-    lax.fori_loop(0, NK // 2, two, 0)
+        prod[...] = both[:256] + (both[256:] + low)
+
+    def combine(quad, prod, groups):
+        for group in groups:
+            row, lane = group // 2 * 8, group % 2 * LANES
+            bins = {}
+            for j, k in enumerate(QUADS[quad]):
+                re, im = (prod[j, r : r + 8, lane : lane + LANES] for r in (row, 128 + row))
+                if k == 0:
+                    bins[0], bins[NK] = (re, None), (im, None)
+                else:
+                    bins[k] = (re, im)
+            for i, one in enumerate(inverse_step(bins, NF)):
+                for j, two in enumerate(inverse_step(one, NF // 2)):
+                    pair = (two[0][0], two[4][0]) if quad == 0 else two[quad]
+                    for part in range(2):
+                        part_ref[quad, i + 2 * j, part, row : row + 8, lane : lane + LANES] = pair[part]
+
+    order = [k for quad in QUADS for k in quad]
+    slot = ((left_a, high_a, low_a), (left_b, high_b, low_b))
+    prods = (prod_a, prod_b)
+    build(order[0], *slot[0])
+    for i in range(NK):
+        multiply(prods[i // 4 % 2].at[i % 4], *slot[i % 2])
+        if i + 1 < NK:
+            build(order[i + 1], *slot[(i + 1) % 2])
+        if i >= 4:
+            combine(i // 4 - 1, prods[(i // 4 - 1) % 2], range(8 * (i % 4), 8 * (i % 4) + 8))
+    combine(3, prods[1], range(32))
     best_ref[...] = jnp.zeros_like(best_ref)
 
     def finish(z, carry):
         row = pl.multiple_of(z * NO, NO)
         here = lax.broadcasted_iota(jnp.int32, (SLAB, LANES), 0) == z
         for lane in range(0, NY, LANES):
-            top = None
-            for o in (0, 8):
-                pairs = [
-                    (
-                        prod_ref[k, pl.ds(row + o, 8), lane : lane + LANES],
-                        prod_ref[k, pl.ds(128 + row + o, 8), lane : lane + LANES],
+            for sub in range(4):
+                top = None
+                for o in (0, 8):
+                    pairs = [
+                        tuple(part_ref[q, sub, p, pl.ds(row + o, 8), lane : lane + LANES] for p in range(2))
+                        for q in range(4)
+                    ]
+                    bins = {0: (pairs[0][0], None), 4: (pairs[0][1], None)}
+                    bins.update({q: pairs[q] for q in range(1, 4)})
+                    rows = inverse(bins, 8, 4)
+                    top = rows if top is None else [jnp.maximum(a, b) for a, b in zip(top, rows)]
+                for m in range(4):
+                    x = 4 * m + sub
+                    largest = jnp.max(top[m], axis=0, keepdims=True)
+                    best_ref[x, :, lane : lane + LANES] = jnp.where(
+                        here, largest, best_ref[x, :, lane : lane + LANES]
                     )
-                    for k in range(NK)
-                ]
-                rows = inverse(unslot(pairs), NF, NF // 2)
-                top = rows if top is None else [jnp.maximum(a, b) for a, b in zip(top, rows)]
-            for x in range(NF // 2):
-                largest = jnp.max(top[x], axis=0, keepdims=True)
-                best_ref[x, :, lane : lane + LANES] = jnp.where(
-                    here, largest, best_ref[x, :, lane : lane + LANES]
-                )
         return carry
 
     lax.fori_loop(0, SLAB, finish, 0)
@@ -364,8 +391,8 @@
         return lax.ppermute(value, "orient", [(i, i ^ mask) for i in range(count)])
 
     right, small = (jnp.asarray(t) for t in filter_tables())
-    normed = call(
-        front_kernel, pltpu.VMEM((TS, TS * TS), f32),
+    normed, token = call(
+        front_kernel, (pltpu.VMEM((TS, TS * TS), f32), pltpu.VMEM((8, LANES), f32)),
         [
             pltpu.VMEM((TS, TS, TS), f32),
             pltpu.VMEM((TS, TS, TS), jnp.int32),
@@ -379,9 +406,11 @@
     window = call(
         window_kernel, pltpu.VMEM((NF, SLAB, NY), f32),
         [pltpu.VMEM((NY // LANES, SLAB, NF, LANES), f32), pltpu.SemaphoreType.DMA((8,))],
-        (normed, volume), [VMEM, HBM], 0, 1 << 19, None,
-    )
-    fan = jnp.broadcast_to(jnp.concatenate([normed, other], axis=0), (8, 2 * TS, TS * TS))
+        (token, volume), [VMEM, HBM], 1 << 31, 1 << 19, 16 * 1024 * 1024,
+    )
+    fan = call(
+        fan_kernel, pltpu.VMEM((8, 2 * TS, TS * TS), f32), [], (normed, other), [VMEM] * 2, 1 << 33, 1 << 18
+    )
     near = [[8 * a + b for a in range(8)] for b in range(8)]
     gathered = lax.all_to_all(
         fan, "orient", 0, 0, tiled=True, axis_index_groups=near
@@ -409,7 +438,9 @@
             pltpu.VMEM((KDIM, NY), bf16),
             pltpu.VMEM((KDIM, NY), bf16),
             pltpu.VMEM((KDIM, NY), bf16),
-            pltpu.VMEM((NK, 256, NY), f32),
+            pltpu.VMEM((4, 256, NY), f32),
+            pltpu.VMEM((4, 256, NY), f32),
+            pltpu.VMEM((4, 4, 2, 128, NY), f32),
             pltpu.VMEM((NF // 2, SLAB, NY), f32),
         ],
         (gathered, spread, high, low), [VMEM] * 4, 1 << 33, 1 << 21,

time: 46.7 us -> 44.2 us (0.946)
  Pallas kernels: 15.1 us -> 11.8 us
  local copies, waits for them, and re-layouts: 0.03 us -> 1.6 us
  other arithmetic: 0.72 us -> 0 us
    pallas_call x6 -> x7, Pallas kernels: 15.1 us -> 11.8 us  [call(): pl.pallas_call(kernel, out_shape=outs, in_specs=specs, out_specs=[VMEM] *...]
    unnamed x4, local copies, waits for them, and re-layouts: 0.01 us -> 1.6 us
    concatenate x1 -> x0, other arithmetic: 0.72 us -> none  [shards(): jnp.concatenate([normed, other], axis=0)]
  transfers between devices with their start and end apart: 6 -> 6, of which waited for: 3 -> 3; matrix products, arithmetic and copies ran while one was open for 2% -> 0% of each run, Pallas kernels for 5% -> 2%
where the time goes in v4:
time: 44.2 us; the launch traced here: 44 us
  starting transfers between devices  15.2 us (34%)
  Pallas kernels  11.8 us (27%)
  blocking collectives  11.7 us (26%)
  waiting for transfers between devices  3.59 us (8%)
  local copies, waits for them, and re-layouts  1.6 us (4%)
    pallas_call x7, Pallas kernels, call(): pl.pallas_call(kernel, out_shape=outs, in_specs=specs, out_specs=[VMEM] *...  11.8 us
    all_to_all x1, blocking collectives, shards(): lax.all_to_all(fan, 'orient', 0, 0, tiled=True, axis_index_groups=near)  11.7 us
    ppermute x4, starting transfers between devices, swap(): return lax.ppermute(value, 'orient', [(i, i ^ mask) for i in range(count)])  10.9 us
    ppermute x4, waiting for transfers between devices, swap(): return lax.ppermute(value, 'orient', [(i, i ^ mask) for i in range(count)])  3.58 us
    ppermute x1, starting transfers between devices, shards(): inside = lax.ppermute(window, 'zslab', [(s, s ^ 1) for s in range(slabs)])  3.56 us
    unnamed x4, local copies, waits for them, and re-layouts  1.6 us
  transfers between devices with their start and end apart: 6, of which 3 were waited for; matrix products, arithmetic and copies ran while one was open for 0% of the time, Pallas kernels for 2%

profile of v4, /device:TPU:2, one launch (start us, length us, event | category | flops | bytes accessed | tf_op | source)
XLA Modules:
  0.0 44.0 jit_solution(14801827157407236155)
XLA Ops:
  0.0 2.3 %shard_map.64 = (f32[16,256]{1,0:T(8,128)S(1)}, f32[8,128]{1,0:T(8,128)S(1)}) custom-call(f32[16,16,16]{2,1,0:T(8,128)} %bitcast.3, s32[16,16,16]{2,1,0:T(8,128)} %wedge_hbm.1, bf16[2,256,512]{2,1,0:T(8,128)(2,1)} %constant.6.clone.right_hbm, f32[2,32,32]{2,1,0:T(8,128)} %constant.7.clone.small_hbm), custom_call_target="tpu_custom_call" | custom-call | flops 4194304 | bytes 1048576 | tf_op jit(solution)/shard_map/pallas_call | solution.py:376
  2.3 7.3 %collective-permute-start.1 = (f32[16,256]{1,0:T(8,128)S(1)}, f32[16,256]{1,0:T(8,128)S(1)}, u32[]{:S(2)}, u32[]{:S(2)}) collective-permute-start(f32[16,256]{1,0:T(8,128)S(1)} %get-tuple-element.17.own_ref), channel_id=1, source_target_pairs={{0,16},{4,20},{8,24},{12,28},{16,0},{20,4},{24,8},{28,12},{32,48},... | collective-permute-start | bytes 49160 | tf_op jit(solution)/shard_map/ppermute | solution.py:391
  9.5 0.0 copy-start
  9.6 1.6 %copy-done = f32[8,256,256]{2,1,0:T(8,128)S(1)} copy-done((f32[8,256,256]{2,1,0:T(8,128)S(1)}, f32[8,256,256]{2,1,0:T(8,128)}, u32[]{:S(2)}) %copy-start) | copy-done | bytes 2097176
  11.1 0.3 shard_map.65.own_ref
  11.4 0.0 copy-start.1
  11.5 0.8 %collective-permute-start.2 = (f32[32,8,256]{2,1,0:T(8,128)S(1)}, f32[32,8,256]{2,1,0:T(8,128)S(1)}, u32[]{:S(2)}, u32[]{:S(2)}) collective-permute-start(f32[32,8,256]{2,1,0:T(8,128)S(1)} %shard_map.65.own_ref), channel_id=1, source_target_pairs={{1,2},{2,1},{5,6},{6,5},{9,10},{10,9},{13,14},{14,13},{17,18},{18,... | collective-permute-start | bytes 786440 | tf_op jit(solution)/shard_map/ppermute | solution.py:421
  12.3 3.6 %collective-permute-start = (f32[32,8,256]{2,1,0:T(8,128)S(1)}, f32[32,8,256]{2,1,0:T(8,128)S(1)}, u32[]{:S(2)}, u32[]{:S(2)}) collective-permute-start(f32[32,8,256]{2,1,0:T(8,128)S(1)} %shard_map.65.own_ref), channel_id=1, source_target_pairs={{0,1},{1,0},{2,3},{3,2},{4,5},{5,4},{6,7},{7,6},{8,9},{9,8},{10,11... | collective-permute-start | bytes 786440 | tf_op jit(solution)/shard_map/ppermute | solution.py:420
  15.8 0.0 collective-permute-done.1.other_ref
  15.9 11.7 %all_to_all.5 = f32[8,32,256]{2,1,0:T(8,128)S(1)} all-to-all(f32[8,32,256]{2,1,0:T(8,128)S(1)} %shard_map.66), channel_id=1, replica_groups={{0,32,64,96,128,160,192,224},{4,36,68,100,132,164,196,228},{8,40,72,104..., dimensions={0} | all-to-all | bytes 524288 | tf_op jit(solution)/shard_map/all_to_all | solution.py:415
  27.6 0.0 collective-permute-done.inside_ref
  27.6 0.0 collective-permute-done.2.across_ref
  27.6 0.5 %shard_map.67 = (bf16[16,128,256]{2,1,0:T(8,128)(2,1)S(1)}, bf16[16,128,256]{2,1,0:T(8,128)(2,1)S(1)}) custom-call(f32[32,8,256]{2,1,0:T(8,128)S(1)} %collective-permute-done.inside_ref, f32[32,8,256]{2,1,0:T(8,128)S(1)} %shard_map.65.own_ref, f32[32,8,256]{2,1,0:T(8,128)S(1)} %collective-permute-done.2.across_ref), custom_call_target="tpu_custom_call" | custom-call | flops 16777216 | bytes 2097152 | tf_op jit(solution)/shard_map/pallas_call | solution.py:376
  28.1 0.0 copy-done.1
  28.1 7.7 %shard_map.68 = (f32[4,8,256]{2,1,0:T(8,128)S(1)}, f32[4,8,256]{2,1,0:T(8,128)S(1)}, f32[4,8,256]{2,1,0:T(8,128)S(1)}, f32[4,8,256]{2,1,0:T(8,128)S(1)}) custom-call(f32[256,256]{1,0:T(8,128)S(1)} %bitcast.2, bf16[256,384]{1,0:T(8,128)(2,1)S(1)} %copy-done.1, bf16[16,128,256]{2,1,0:T(8,128)(2,1)S(1)} %get-tuple-element.20.high_ref, ...), custom_call_target="tpu_custom_call" | custom-call | flops 8589934592 | bytes 2097152 | tf_op jit(solution)/shard_map/pallas_call | solution.py:376
  35.8 1.6 %collective-permute-start.4 = (f32[4,8,256]{2,1,0:T(8,128)S(1)}, f32[4,8,256]{2,1,0:T(8,128)S(1)}, u32[]{:S(2)}, u32[]{:S(2)}) collective-permute-start(f32[4,8,256]{2,1,0:T(8,128)S(1)} %get-tuple-element.25), channel_id=1, source_target_pairs={{0,8},{4,12},{8,0},{12,4},{16,24},{20,28},{24,16},{28,20},{32,40},... | collective-permute-start | bytes 98312 | tf_op jit(solution)/shard_map/ppermute | solution.py:391
  37.3 1.9 %collective-permute-start.5 = (f32[4,8,256]{2,1,0:T(8,128)S(1)}, f32[4,8,256]{2,1,0:T(8,128)S(1)}, u32[]{:S(2)}, u32[]{:S(2)}) collective-permute-start(f32[4,8,256]{2,1,0:T(8,128)S(1)} %get-tuple-element.26), channel_id=1, source_target_pairs={{0,12},{4,8},{8,4},{12,0},{16,28},{20,24},{24,20},{28,16},{32,44},... | collective-permute-start | bytes 98312 | tf_op jit(solution)/shard_map/ppermute | solution.py:391
  39.2 0.1 collective-permute-start.3
  39.4 0.5 %shard_map.69.scale_ref = f32[4,8,256]{2,1,0:T(8,128)S(1)} custom-call(f32[32,8,256]{2,1,0:T(8,128)S(1)} %collective-permute-done.inside_ref, f32[32,8,256]{2,1,0:T(8,128)S(1)} %shard_map.65.own_ref, f32[32,8,256]{2,1,0:T(8,128)S(1)} %collective-permute-done.2.across_ref), custom_call_target="tpu_custom_call" | custom-call | flops 4194304 | bytes 1048576 | tf_op jit(solution)/shard_map/pallas_call | solution.py:376
  39.8 0.9 %collective-permute-done.4.c_ref = f32[4,8,256]{2,1,0:T(8,128)S(1)} collective-permute-done((f32[4,8,256]{2,1,0:T(8,128)S(1)}, f32[4,8,256]{2,1,0:T(8,128)S(1)}, u32[]{:S(2)}, u32[]{:S(2)}) %collective-permute-start.4) | collective-permute-done | bytes 32800 | tf_op jit(solution)/shard_map/ppermute | solution.py:391
  40.7 2.3 %collective-permute-done.5.d_ref = f32[4,8,256]{2,1,0:T(8,128)S(1)} collective-permute-done((f32[4,8,256]{2,1,0:T(8,128)S(1)}, f32[4,8,256]{2,1,0:T(8,128)S(1)}, u32[]{:S(2)}, u32[]{:S(2)}) %collective-permute-start.5) | collective-permute-done | bytes 32800 | tf_op jit(solution)/shard_map/ppermute | solution.py:391
  43.1 0.3 collective-permute-done.3.b_ref
  43.4 0.6 %shard_map.70 = f32[8,4,256]{2,1,0:T(4,128)} custom-call(f32[4,8,256]{2,1,0:T(8,128)S(1)} %shard_map.69.scale_ref, f32[4,8,256]{2,1,0:T(8,128)S(1)} %get-tuple-element.24.a_ref, f32[4,8,256]{2,1,0:T(8,128)S(1)} %collective-permute-done.3.b_ref, f32[4,8,256]{2,1,0:T(8,128)S(1)} %collective-permute-done.4.c_ref, f32[4,8,256]{2,1,0:T(8,128)S(1)} %collective-permute-done.5.d_ref), custom_call_target="tpu_custom_call" | custom-call | flops 65536 | bytes 262144 | tf_op jit(solution)/shard_map/pallas_call | solution.py:376
  (1 shorter events, 0.0 us)
Async XLA Ops:
  2.3 13.6 %collective-permute-start.1 = (f32[16,256]{1,0:T(8,128)S(1)}, f32[16,256]{1,0:T(8,128)S(1)}, u32[]{:S(2)}, u32[]{:S(2)}) collective-permute-start(f32[16,256]{1,0:T(8,128)S(1)} %get-tuple-element.17.own_ref), channel_id=1, source_target_pairs={{0,16},{4,20},{8,24},{12,28},{16,0},{20,4},{24,8},{28,12},{32,48},... | collective-permute-start | bytes 49160 | tf_op jit(solution)/shard_map/ppermute | solution.py:391
  9.5 1.6 %copy-start = (f32[8,256,256]{2,1,0:T(8,128)S(1)}, f32[8,256,256]{2,1,0:T(8,128)}, u32[]{:S(2)}) copy-start(f32[8,256,256]{2,1,0:T(8,128)} %volume_hbm.1) | copy-start | bytes 6291460
  11.4 16.7 %copy-start.1 = (bf16[256,384]{1,0:T(8,128)(2,1)S(1)}, bf16[256,384]{1,0:T(8,128)(2,1)}, u32[]{:S(2)}) copy-start(bf16[256,384]{1,0:T(8,128)(2,1)} %constant.8.clone.spread_ref) | copy-start | bytes 589828
  11.5 16.1 %collective-permute-start.2 = (f32[32,8,256]{2,1,0:T(8,128)S(1)}, f32[32,8,256]{2,1,0:T(8,128)S(1)}, u32[]{:S(2)}, u32[]{:S(2)}) collective-permute-start(f32[32,8,256]{2,1,0:T(8,128)S(1)} %shard_map.65.own_ref), channel_id=1, source_target_pairs={{1,2},{2,1},{5,6},{6,5},{9,10},{10,9},{13,14},{14,13},{17,18},{18,... | collective-permute-start | bytes 786440 | tf_op jit(solution)/shard_map/ppermute | solution.py:421
  12.3 15.3 %collective-permute-start = (f32[32,8,256]{2,1,0:T(8,128)S(1)}, f32[32,8,256]{2,1,0:T(8,128)S(1)}, u32[]{:S(2)}, u32[]{:S(2)}) collective-permute-start(f32[32,8,256]{2,1,0:T(8,128)S(1)} %shard_map.65.own_ref), channel_id=1, source_target_pairs={{0,1},{1,0},{2,3},{3,2},{4,5},{5,4},{6,7},{7,6},{8,9},{9,8},{10,11... | collective-permute-start | bytes 786440 | tf_op jit(solution)/shard_map/ppermute | solution.py:420
  35.8 4.9 %collective-permute-start.4 = (f32[4,8,256]{2,1,0:T(8,128)S(1)}, f32[4,8,256]{2,1,0:T(8,128)S(1)}, u32[]{:S(2)}, u32[]{:S(2)}) collective-permute-start(f32[4,8,256]{2,1,0:T(8,128)S(1)} %get-tuple-element.25), channel_id=1, source_target_pairs={{0,8},{4,12},{8,0},{12,4},{16,24},{20,28},{24,16},{28,20},{32,40},... | collective-permute-start | bytes 98312 | tf_op jit(solution)/shard_map/ppermute | solution.py:391
  37.3 5.7 %collective-permute-start.5 = (f32[4,8,256]{2,1,0:T(8,128)S(1)}, f32[4,8,256]{2,1,0:T(8,128)S(1)}, u32[]{:S(2)}, u32[]{:S(2)}) collective-permute-start(f32[4,8,256]{2,1,0:T(8,128)S(1)} %get-tuple-element.26), channel_id=1, source_target_pairs={{0,12},{4,8},{8,4},{12,0},{16,28},{20,24},{24,20},{28,16},{32,44},... | collective-permute-start | bytes 98312 | tf_op jit(solution)/shard_map/ppermute | solution.py:391
  39.2 4.2 %collective-permute-start.3 = (f32[4,8,256]{2,1,0:T(8,128)S(1)}, f32[4,8,256]{2,1,0:T(8,128)S(1)}, u32[]{:S(2)}, u32[]{:S(2)}) collective-permute-start(f32[4,8,256]{2,1,0:T(8,128)S(1)} %get-tuple-element.22), channel_id=1, source_target_pairs={{0,4},{4,0},{8,12},{12,8},{16,20},{20,16},{24,28},{28,24},{32,36},... | collective-permute-start | bytes 98312 | tf_op jit(solution)/shard_map/ppermute | solution.py:391

commit v5 on v4

--- a/solution.py
+++ b/solution.py
@@ -133,8 +133,8 @@
 
 
 def front_kernel(
-    template_hbm, wedge_hbm, right_hbm, small_hbm, out_ref, token_ref,
-    template_ref, wedge_ref, right_ref, small_ref, sems,
+    template_hbm, wedge_hbm, volume_hbm, right_hbm, small_hbm, out_ref, window_ref,
+    template_ref, wedge_ref, right_ref, small_ref, piece_ref, sems,
 ):
     width = TS * TS
     copies = [
@@ -145,6 +145,19 @@
     ]
     for copy in copies:
         copy.start()
+    rows = volume_hbm.shape[1]
+    first = lax.axis_index("orient") // GROUP * 16 + (rows - HALF)
+    pieces = []
+    for j in range(NF // 8):
+        at = pl.multiple_of(lax.rem(first + 8 * j, rows), 8)
+        for h in range(NY // LANES):
+            copy = pltpu.make_async_copy(
+                volume_hbm.at[:, pl.ds(at, 8), pl.ds(h * LANES, LANES)],
+                piece_ref.at[h, :, pl.ds(8 * j, 8), :],
+                sems.at[4 + len(pieces)],
+            )
+            copy.start()
+            pieces.append(copy)
 
     def flat(ref):
         return jnp.concatenate([ref[c].astype(jnp.float32) for c in range(TS)], axis=1)
@@ -170,23 +183,6 @@
     filt = filt * (1.0 / float(TS**3))
     centered = filt - jnp.sum(filt) * (1.0 / float(TS**3))
     out_ref[...] = centered / jnp.sqrt(jnp.sum(centered * centered) + 1e-05)
-    token_ref[...] = jnp.zeros_like(token_ref)
-
-
-def window_kernel(after_ref, volume_hbm, window_ref, piece_ref, sems):
-    rows = volume_hbm.shape[1]
-    first = lax.axis_index("orient") // GROUP * 16 + (rows - HALF)
-    pieces = []
-    for j in range(NF // 8):
-        at = pl.multiple_of(lax.rem(first + 8 * j, rows), 8)
-        for h in range(NY // LANES):
-            copy = pltpu.make_async_copy(
-                volume_hbm.at[:, pl.ds(at, 8), pl.ds(h * LANES, LANES)],
-                piece_ref.at[h, :, pl.ds(8 * j, 8), :],
-                sems.at[len(pieces)],
-            )
-            copy.start()
-            pieces.append(copy)
     for copy in pieces:
         copy.wait()
     flat_piece = piece_ref.reshape(NY // LANES, SLAB * NF, LANES)
@@ -391,23 +387,20 @@
         return lax.ppermute(value, "orient", [(i, i ^ mask) for i in range(count)])
 
     right, small = (jnp.asarray(t) for t in filter_tables())
-    normed, token = call(
-        front_kernel, (pltpu.VMEM((TS, TS * TS), f32), pltpu.VMEM((8, LANES), f32)),
+    normed, window = call(
+        front_kernel,
+        (pltpu.VMEM((TS, TS * TS), f32), pltpu.VMEM((NF, SLAB, NY), f32)),
         [
             pltpu.VMEM((TS, TS, TS), f32),
             pltpu.VMEM((TS, TS, TS), jnp.int32),
             pltpu.VMEM(right.shape, bf16),
             pltpu.VMEM(small.shape, f32),
-            pltpu.SemaphoreType.DMA((4,)),
+            pltpu.VMEM((NY // LANES, SLAB, NF, LANES), f32),
+            pltpu.SemaphoreType.DMA((12,)),
         ],
-        (templates[0], wedge, right, small), [HBM] * 4, 1 << 22, 1 << 20, None,
+        (templates[0], wedge, volume, right, small), [HBM] * 5, 1 << 22, 1 << 20, None,
     )
     other = swap(normed, 4)
-    window = call(
-        window_kernel, pltpu.VMEM((NF, SLAB, NY), f32),
-        [pltpu.VMEM((NY // LANES, SLAB, NF, LANES), f32), pltpu.SemaphoreType.DMA((8,))],
-        (token, volume), [VMEM, HBM], 1 << 31, 1 << 19, 16 * 1024 * 1024,
-    )
     fan = call(
         fan_kernel, pltpu.VMEM((8, 2 * TS, TS * TS), f32), [], (normed, other), [VMEM] * 2, 1 << 33, 1 << 18
     )
@@ -418,7 +411,8 @@
 
     slabs = lax.axis_size("zslab")
     inside = lax.ppermute(window, "zslab", [(s, s ^ 1) for s in range(slabs)])
-    across = lax.ppermute(window, "zslab", [(1, 2), (2, 1)])
+    later, inside = lax.optimization_barrier((window, inside))
+    across = lax.ppermute(later, "zslab", [(1, 2), (2, 1)])
     inside, gathered = lax.optimization_barrier((inside, gathered))
     spectrum = jax.ShapeDtypeStruct((NK, 128, NY), bf16)
     high, low = call(

time: 44.2 us -> 41.7 us (0.943)
  the two profiles are of different devices: /device:TPU:2 before, /device:TPU:4 now
where the time goes in v5:
time: 41.7 us; the launch traced here: 41.6 us
  starting transfers between devices  13.1 us (31%)
  blocking collectives  13 us (31%)
  Pallas kernels  11.8 us (28%)
  waiting for transfers between devices  3.59 us (9%)
    all_to_all x1, blocking collectives, shards(): lax.all_to_all(fan, 'orient', 0, 0, tiled=True, axis_index_groups=near)  13 us
    pallas_call x6, Pallas kernels, call(): pl.pallas_call(kernel, out_shape=outs, in_specs=specs, out_specs=[VMEM] *...  11.8 us
    ppermute x4, starting transfers between devices, swap(): return lax.ppermute(value, 'orient', [(i, i ^ mask) for i in range(count)])  10.9 us
    ppermute x4, waiting for transfers between devices, swap(): return lax.ppermute(value, 'orient', [(i, i ^ mask) for i in range(count)])  3.58 us
    ppermute x1, starting transfers between devices, shards(): across = lax.ppermute(later, 'zslab', [(1, 2), (2, 1)])  2.16 us
  transfers between devices with their start and end apart: 6, of which 3 were waited for; matrix products, arithmetic and copies ran while one was open for 0% of the time, Pallas kernels for 1%

profile of v5, /device:TPU:4, one launch (start us, length us, event | category | flops | bytes accessed | tf_op | source)
XLA Modules:
  0.0 41.6 jit_solution(4054416771658338765)
XLA Ops:
  0.0 2.5 %shard_map.64 = (f32[16,256]{1,0:T(8,128)S(1)}, f32[32,8,256]{2,1,0:T(8,128)S(1)}) custom-call(f32[16,16,16]{2,1,0:T(8,128)} %bitcast.3, s32[16,16,16]{2,1,0:T(8,128)} %wedge_hbm.1, f32[8,256,256]{2,1,0:T(8,128)} %volume_hbm.1, bf16[2,256,512]{2,1,0:T(8,128)(2,1)} %constant.6.clone.right_hbm, f32[2,32,32]{2,1,0:T(8,128)} %constant.7.clone.small_hbm), custom_call_target="tpu_custom_call" | custom-call | flops 4194304 | bytes 1048576 | tf_op jit(solution)/shard_map/pallas_call | solution.py:372
  2.5 0.1 collective-permute-start
  2.6 0.0 copy-start
  2.6 7.3 %collective-permute-start.1 = (f32[16,256]{1,0:T(8,128)S(1)}, f32[16,256]{1,0:T(8,128)S(1)}, u32[]{:S(2)}, u32[]{:S(2)}) collective-permute-start(f32[16,256]{1,0:T(8,128)S(1)} %get-tuple-element.20.own_ref), channel_id=1, source_target_pairs={{0,16},{4,20},{8,24},{12,28},{16,0},{20,4},{24,8},{28,12},{32,48},... | collective-permute-start | bytes 49160 | tf_op jit(solution)/shard_map/ppermute | solution.py:387
  9.9 0.0 collective-permute-done.inside_ref
  9.9 2.2 %collective-permute-start.2 = (f32[32,8,256]{2,1,0:T(8,128)S(1)}, f32[32,8,256]{2,1,0:T(8,128)S(1)}, u32[]{:S(2)}, u32[]{:S(2)}) collective-permute-start(f32[32,8,256]{2,1,0:T(8,128)S(1)} %get-tuple-element.23.own_ref), channel_id=1, source_target_pairs={{1,2},{2,1},{5,6},{6,5},{9,10},{10,9},{13,14},{14,13},{17,18},{18,... | collective-permute-start | bytes 786440 | tf_op jit(solution)/shard_map/ppermute | solution.py:415
  12.1 0.0 collective-permute-done.1.other_ref
  12.1 13.0 %all_to_all.5 = f32[8,32,256]{2,1,0:T(8,128)S(1)} all-to-all(f32[8,32,256]{2,1,0:T(8,128)S(1)} %shard_map.65), channel_id=1, replica_groups={{0,32,64,96,128,160,192,224},{4,36,68,100,132,164,196,228},{8,40,72,104..., dimensions={0} | all-to-all | bytes 524288 | tf_op jit(solution)/shard_map/all_to_all | solution.py:408
  25.1 0.0 collective-permute-done.2.across_ref
  25.1 0.5 %shard_map.66 = (bf16[16,128,256]{2,1,0:T(8,128)(2,1)S(1)}, bf16[16,128,256]{2,1,0:T(8,128)(2,1)S(1)}) custom-call(f32[32,8,256]{2,1,0:T(8,128)S(1)} %collective-permute-done.inside_ref, f32[32,8,256]{2,1,0:T(8,128)S(1)} %get-tuple-element.23.own_ref, f32[32,8,256]{2,1,0:T(8,128)S(1)} %collective-permute-done.2.across_ref), custom_call_target="tpu_custom_call" | custom-call | flops 16777216 | bytes 2097152 | tf_op jit(solution)/shard_map/pallas_call | solution.py:372
  25.6 0.0 copy-done
  25.6 7.7 %shard_map.67 = (f32[4,8,256]{2,1,0:T(8,128)S(1)}, f32[4,8,256]{2,1,0:T(8,128)S(1)}, f32[4,8,256]{2,1,0:T(8,128)S(1)}, f32[4,8,256]{2,1,0:T(8,128)S(1)}) custom-call(f32[256,256]{1,0:T(8,128)S(1)} %bitcast.2, bf16[256,384]{1,0:T(8,128)(2,1)S(1)} %copy-done, bf16[16,128,256]{2,1,0:T(8,128)(2,1)S(1)} %get-tuple-element.24.high_ref, ...), custom_call_target="tpu_custom_call" | custom-call | flops 8589934592 | bytes 2097152 | tf_op jit(solution)/shard_map/pallas_call | solution.py:372
  33.3 1.6 %collective-permute-start.4 = (f32[4,8,256]{2,1,0:T(8,128)S(1)}, f32[4,8,256]{2,1,0:T(8,128)S(1)}, u32[]{:S(2)}, u32[]{:S(2)}) collective-permute-start(f32[4,8,256]{2,1,0:T(8,128)S(1)} %get-tuple-element.29), channel_id=1, source_target_pairs={{0,8},{4,12},{8,0},{12,4},{16,24},{20,28},{24,16},{28,20},{32,40},... | collective-permute-start | bytes 98312 | tf_op jit(solution)/shard_map/ppermute | solution.py:387
  34.9 1.9 %collective-permute-start.5 = (f32[4,8,256]{2,1,0:T(8,128)S(1)}, f32[4,8,256]{2,1,0:T(8,128)S(1)}, u32[]{:S(2)}, u32[]{:S(2)}) collective-permute-start(f32[4,8,256]{2,1,0:T(8,128)S(1)} %get-tuple-element.30), channel_id=1, source_target_pairs={{0,12},{4,8},{8,4},{12,0},{16,28},{20,24},{24,20},{28,16},{32,44},... | collective-permute-start | bytes 98312 | tf_op jit(solution)/shard_map/ppermute | solution.py:387
  36.8 0.1 collective-permute-start.3
  36.9 0.5 %shard_map.68.scale_ref = f32[4,8,256]{2,1,0:T(8,128)S(1)} custom-call(f32[32,8,256]{2,1,0:T(8,128)S(1)} %collective-permute-done.inside_ref, f32[32,8,256]{2,1,0:T(8,128)S(1)} %get-tuple-element.23.own_ref, f32[32,8,256]{2,1,0:T(8,128)S(1)} %collective-permute-done.2.across_ref), custom_call_target="tpu_custom_call" | custom-call | flops 4194304 | bytes 1048576 | tf_op jit(solution)/shard_map/pallas_call | solution.py:372
  37.4 0.9 %collective-permute-done.4.c_ref = f32[4,8,256]{2,1,0:T(8,128)S(1)} collective-permute-done((f32[4,8,256]{2,1,0:T(8,128)S(1)}, f32[4,8,256]{2,1,0:T(8,128)S(1)}, u32[]{:S(2)}, u32[]{:S(2)}) %collective-permute-start.4) | collective-permute-done | bytes 32800 | tf_op jit(solution)/shard_map/ppermute | solution.py:387
  38.2 2.4 %collective-permute-done.5.d_ref = f32[4,8,256]{2,1,0:T(8,128)S(1)} collective-permute-done((f32[4,8,256]{2,1,0:T(8,128)S(1)}, f32[4,8,256]{2,1,0:T(8,128)S(1)}, u32[]{:S(2)}, u32[]{:S(2)}) %collective-permute-start.5) | collective-permute-done | bytes 32800 | tf_op jit(solution)/shard_map/ppermute | solution.py:387
  40.6 0.3 collective-permute-done.3.b_ref
  40.9 0.6 %shard_map.69 = f32[8,4,256]{2,1,0:T(4,128)} custom-call(f32[4,8,256]{2,1,0:T(8,128)S(1)} %shard_map.68.scale_ref, f32[4,8,256]{2,1,0:T(8,128)S(1)} %get-tuple-element.28.a_ref, f32[4,8,256]{2,1,0:T(8,128)S(1)} %collective-permute-done.3.b_ref, f32[4,8,256]{2,1,0:T(8,128)S(1)} %collective-permute-done.4.c_ref, f32[4,8,256]{2,1,0:T(8,128)S(1)} %collective-permute-done.5.d_ref), custom_call_target="tpu_custom_call" | custom-call | flops 65536 | bytes 262144 | tf_op jit(solution)/shard_map/pallas_call | solution.py:372
  (1 shorter events, 0.0 us)
Async XLA Ops:
  2.5 7.4 %collective-permute-start = (f32[32,8,256]{2,1,0:T(8,128)S(1)}, f32[32,8,256]{2,1,0:T(8,128)S(1)}, u32[]{:S(2)}, u32[]{:S(2)}) collective-permute-start(f32[32,8,256]{2,1,0:T(8,128)S(1)} %get-tuple-element.23.own_ref), channel_id=1, source_target_pairs={{0,1},{1,0},{2,3},{3,2},{4,5},{5,4},{6,7},{7,6},{8,9},{9,8},{10,11... | collective-permute-start | bytes 786440 | tf_op jit(solution)/shard_map/ppermute | solution.py:413
  2.6 23.0 %copy-start = (bf16[256,384]{1,0:T(8,128)(2,1)S(1)}, bf16[256,384]{1,0:T(8,128)(2,1)}, u32[]{:S(2)}) copy-start(bf16[256,384]{1,0:T(8,128)(2,1)} %constant.8.clone.spread_ref) | copy-start | bytes 589828
  2.6 9.4 %collective-permute-start.1 = (f32[16,256]{1,0:T(8,128)S(1)}, f32[16,256]{1,0:T(8,128)S(1)}, u32[]{:S(2)}, u32[]{:S(2)}) collective-permute-start(f32[16,256]{1,0:T(8,128)S(1)} %get-tuple-element.20.own_ref), channel_id=1, source_target_pairs={{0,16},{4,20},{8,24},{12,28},{16,0},{20,4},{24,8},{28,12},{32,48},... | collective-permute-start | bytes 49160 | tf_op jit(solution)/shard_map/ppermute | solution.py:387
  9.9 15.2 %collective-permute-start.2 = (f32[32,8,256]{2,1,0:T(8,128)S(1)}, f32[32,8,256]{2,1,0:T(8,128)S(1)}, u32[]{:S(2)}, u32[]{:S(2)}) collective-permute-start(f32[32,8,256]{2,1,0:T(8,128)S(1)} %get-tuple-element.23.own_ref), channel_id=1, source_target_pairs={{1,2},{2,1},{5,6},{6,5},{9,10},{10,9},{13,14},{14,13},{17,18},{18,... | collective-permute-start | bytes 786440 | tf_op jit(solution)/shard_map/ppermute | solution.py:415
  33.3 4.9 %collective-permute-start.4 = (f32[4,8,256]{2,1,0:T(8,128)S(1)}, f32[4,8,256]{2,1,0:T(8,128)S(1)}, u32[]{:S(2)}, u32[]{:S(2)}) collective-permute-start(f32[4,8,256]{2,1,0:T(8,128)S(1)} %get-tuple-element.29), channel_id=1, source_target_pairs={{0,8},{4,12},{8,0},{12,4},{16,24},{20,28},{24,16},{28,20},{32,40},... | collective-permute-start | bytes 98312 | tf_op jit(solution)/shard_map/ppermute | solution.py:387
  34.9 5.7 %collective-permute-start.5 = (f32[4,8,256]{2,1,0:T(8,128)S(1)}, f32[4,8,256]{2,1,0:T(8,128)S(1)}, u32[]{:S(2)}, u32[]{:S(2)}) collective-permute-start(f32[4,8,256]{2,1,0:T(8,128)S(1)} %get-tuple-element.30), channel_id=1, source_target_pairs={{0,12},{4,8},{8,4},{12,0},{16,28},{20,24},{24,20},{28,16},{32,44},... | collective-permute-start | bytes 98312 | tf_op jit(solution)/shard_map/ppermute | solution.py:387
  36.8 4.2 %collective-permute-start.3 = (f32[4,8,256]{2,1,0:T(8,128)S(1)}, f32[4,8,256]{2,1,0:T(8,128)S(1)}, u32[]{:S(2)}, u32[]{:S(2)}) collective-permute-start(f32[4,8,256]{2,1,0:T(8,128)S(1)} %get-tuple-element.26), channel_id=1, source_target_pairs={{0,4},{4,0},{8,12},{12,8},{16,20},{20,16},{24,28},{28,24},{32,36},... | collective-permute-start | bytes 98312 | tf_op jit(solution)/shard_map/ppermute | solution.py:387

commit v6 on v5

--- a/solution.py
+++ b/solution.py
@@ -218,7 +218,7 @@
             )
         return carry
 
-    lax.fori_loop(0, NK, split, 0)
+    lax.fori_loop(0, NK, split, 0, unroll=4)
 
 
 def scale_kernel(inside_ref, own_ref, across_ref, scale_ref):
@@ -356,7 +356,7 @@
                     )
         return carry
 
-    lax.fori_loop(0, SLAB, finish, 0)
+    lax.fori_loop(0, SLAB, finish, 0, unroll=2)
     mine = lax.rem(lax.axis_index("orient"), GROUP)
     for m, ref in enumerate((out0_ref, out1_ref, out2_ref, out3_ref)):
         ref[...] = best_ref[pl.ds((mine ^ m) * STRIP, STRIP)]
@@ -400,7 +400,7 @@
         ],
         (templates[0], wedge, volume, right, small), [HBM] * 5, 1 << 22, 1 << 20, None,
     )
-    other = swap(normed, 4)
+    other = swap(normed, 6)
     fan = call(
         fan_kernel, pltpu.VMEM((8, 2 * TS, TS * TS), f32), [], (normed, other), [VMEM] * 2, 1 << 33, 1 << 18
     )

time: 41.7 us -> 41 us (0.983)
  starting transfers between devices: 13.1 us -> 12.2 us
    ppermute x4, starting transfers between devices: 10.9 us -> 9.96 us  [swap(): return lax.ppermute(value, 'orient', [(i, i ^ mask) for i in range(count)])]
where the time goes in v6:
time: 41 us; the launch traced here: 40.6 us
  blocking collectives  13 us (32%)
  starting transfers between devices  12.2 us (30%)
  Pallas kernels  11.7 us (29%)
  waiting for transfers between devices  3.57 us (9%)
    all_to_all x1, blocking collectives, shards(): lax.all_to_all(fan, 'orient', 0, 0, tiled=True, axis_index_groups=near)  13 us
    pallas_call x6, Pallas kernels, call(): pl.pallas_call(kernel, out_shape=outs, in_specs=specs, out_specs=[VMEM] *...  11.7 us
    ppermute x4, starting transfers between devices, swap(): return lax.ppermute(value, 'orient', [(i, i ^ mask) for i in range(count)])  9.96 us
    ppermute x4, waiting for transfers between devices, swap(): return lax.ppermute(value, 'orient', [(i, i ^ mask) for i in range(count)])  3.57 us
    ppermute x1, starting transfers between devices, shards(): across = lax.ppermute(later, 'zslab', [(1, 2), (2, 1)])  2.16 us
  transfers between devices with their start and end apart: 6, of which 3 were waited for; matrix products, arithmetic and copies ran while one was open for 0% of the time, Pallas kernels for 1%

profile of v6, /device:TPU:4, one launch (start us, length us, event | category | flops | bytes accessed | tf_op | source)
XLA Modules:
  0.0 40.6 jit_solution(188227285273251166)
XLA Ops:
  0.0 2.5 %shard_map.64 = (f32[16,256]{1,0:T(8,128)S(1)}, f32[32,8,256]{2,1,0:T(8,128)S(1)}) custom-call(f32[16,16,16]{2,1,0:T(8,128)} %bitcast.3, s32[16,16,16]{2,1,0:T(8,128)} %wedge_hbm.1, f32[8,256,256]{2,1,0:T(8,128)} %volume_hbm.1, bf16[2,256,512]{2,1,0:T(8,128)(2,1)} %constant.6.clone.right_hbm, f32[2,32,32]{2,1,0:T(8,128)} %constant.7.clone.small_hbm), custom_call_target="tpu_custom_call" | custom-call | flops 4194304 | bytes 1048576 | tf_op jit(solution)/shard_map/pallas_call | solution.py:372
  2.5 0.1 collective-permute-start
  2.6 0.0 copy-start
  2.6 6.4 %collective-permute-start.1 = (f32[16,256]{1,0:T(8,128)S(1)}, f32[16,256]{1,0:T(8,128)S(1)}, u32[]{:S(2)}, u32[]{:S(2)}) collective-permute-start(f32[16,256]{1,0:T(8,128)S(1)} %get-tuple-element.20.own_ref), channel_id=1, source_target_pairs={{0,24},{4,28},{8,16},{12,20},{16,8},{20,12},{24,0},{28,4},{32,56},... | collective-permute-start | bytes 49160 | tf_op jit(solution)/shard_map/ppermute | solution.py:387
  9.0 0.0 collective-permute-done.inside_ref
  9.0 2.2 %collective-permute-start.2 = (f32[32,8,256]{2,1,0:T(8,128)S(1)}, f32[32,8,256]{2,1,0:T(8,128)S(1)}, u32[]{:S(2)}, u32[]{:S(2)}) collective-permute-start(f32[32,8,256]{2,1,0:T(8,128)S(1)} %get-tuple-element.23.own_ref), channel_id=1, source_target_pairs={{1,2},{2,1},{5,6},{6,5},{9,10},{10,9},{13,14},{14,13},{17,18},{18,... | collective-permute-start | bytes 786440 | tf_op jit(solution)/shard_map/ppermute | solution.py:415
  11.2 0.0 collective-permute-done.1.other_ref
  11.2 13.0 %all_to_all.5 = f32[8,32,256]{2,1,0:T(8,128)S(1)} all-to-all(f32[8,32,256]{2,1,0:T(8,128)S(1)} %shard_map.65), channel_id=1, replica_groups={{0,32,64,96,128,160,192,224},{4,36,68,100,132,164,196,228},{8,40,72,104..., dimensions={0} | all-to-all | bytes 524288 | tf_op jit(solution)/shard_map/all_to_all | solution.py:408
  24.2 0.0 collective-permute-done.2.across_ref
  24.2 0.4 %shard_map.66 = (bf16[16,128,256]{2,1,0:T(8,128)(2,1)S(1)}, bf16[16,128,256]{2,1,0:T(8,128)(2,1)S(1)}) custom-call(f32[32,8,256]{2,1,0:T(8,128)S(1)} %collective-permute-done.inside_ref, f32[32,8,256]{2,1,0:T(8,128)S(1)} %get-tuple-element.23.own_ref, f32[32,8,256]{2,1,0:T(8,128)S(1)} %collective-permute-done.2.across_ref), custom_call_target="tpu_custom_call" | custom-call | flops 16777216 | bytes 2097152 | tf_op jit(solution)/shard_map/pallas_call | solution.py:372
  24.7 0.0 copy-done
  24.7 7.6 %shard_map.67 = (f32[4,8,256]{2,1,0:T(8,128)S(1)}, f32[4,8,256]{2,1,0:T(8,128)S(1)}, f32[4,8,256]{2,1,0:T(8,128)S(1)}, f32[4,8,256]{2,1,0:T(8,128)S(1)}) custom-call(f32[256,256]{1,0:T(8,128)S(1)} %bitcast.2, bf16[256,384]{1,0:T(8,128)(2,1)S(1)} %copy-done, bf16[16,128,256]{2,1,0:T(8,128)(2,1)S(1)} %get-tuple-element.24.high_ref, ...), custom_call_target="tpu_custom_call" | custom-call | flops 8589934592 | bytes 2097152 | tf_op jit(solution)/shard_map/pallas_call | solution.py:372
  32.3 1.5 %collective-permute-start.4 = (f32[4,8,256]{2,1,0:T(8,128)S(1)}, f32[4,8,256]{2,1,0:T(8,128)S(1)}, u32[]{:S(2)}, u32[]{:S(2)}) collective-permute-start(f32[4,8,256]{2,1,0:T(8,128)S(1)} %get-tuple-element.29), channel_id=1, source_target_pairs={{0,8},{4,12},{8,0},{12,4},{16,24},{20,28},{24,16},{28,20},{32,40},... | collective-permute-start | bytes 98312 | tf_op jit(solution)/shard_map/ppermute | solution.py:387
  33.9 1.9 %collective-permute-start.5 = (f32[4,8,256]{2,1,0:T(8,128)S(1)}, f32[4,8,256]{2,1,0:T(8,128)S(1)}, u32[]{:S(2)}, u32[]{:S(2)}) collective-permute-start(f32[4,8,256]{2,1,0:T(8,128)S(1)} %get-tuple-element.30), channel_id=1, source_target_pairs={{0,12},{4,8},{8,4},{12,0},{16,28},{20,24},{24,20},{28,16},{32,44},... | collective-permute-start | bytes 98312 | tf_op jit(solution)/shard_map/ppermute | solution.py:387
  35.8 0.1 collective-permute-start.3
  35.9 0.5 %shard_map.68.scale_ref = f32[4,8,256]{2,1,0:T(8,128)S(1)} custom-call(f32[32,8,256]{2,1,0:T(8,128)S(1)} %collective-permute-done.inside_ref, f32[32,8,256]{2,1,0:T(8,128)S(1)} %get-tuple-element.23.own_ref, f32[32,8,256]{2,1,0:T(8,128)S(1)} %collective-permute-done.2.across_ref), custom_call_target="tpu_custom_call" | custom-call | flops 4194304 | bytes 1048576 | tf_op jit(solution)/shard_map/pallas_call | solution.py:372
  36.4 0.9 %collective-permute-done.4.c_ref = f32[4,8,256]{2,1,0:T(8,128)S(1)} collective-permute-done((f32[4,8,256]{2,1,0:T(8,128)S(1)}, f32[4,8,256]{2,1,0:T(8,128)S(1)}, u32[]{:S(2)}, u32[]{:S(2)}) %collective-permute-start.4) | collective-permute-done | bytes 32800 | tf_op jit(solution)/shard_map/ppermute | solution.py:387
  37.2 2.4 %collective-permute-done.5.d_ref = f32[4,8,256]{2,1,0:T(8,128)S(1)} collective-permute-done((f32[4,8,256]{2,1,0:T(8,128)S(1)}, f32[4,8,256]{2,1,0:T(8,128)S(1)}, u32[]{:S(2)}, u32[]{:S(2)}) %collective-permute-start.5) | collective-permute-done | bytes 32800 | tf_op jit(solution)/shard_map/ppermute | solution.py:387
  39.6 0.3 collective-permute-done.3.b_ref
  39.9 0.6 %shard_map.69 = f32[8,4,256]{2,1,0:T(4,128)} custom-call(f32[4,8,256]{2,1,0:T(8,128)S(1)} %shard_map.68.scale_ref, f32[4,8,256]{2,1,0:T(8,128)S(1)} %get-tuple-element.28.a_ref, f32[4,8,256]{2,1,0:T(8,128)S(1)} %collective-permute-done.3.b_ref, f32[4,8,256]{2,1,0:T(8,128)S(1)} %collective-permute-done.4.c_ref, f32[4,8,256]{2,1,0:T(8,128)S(1)} %collective-permute-done.5.d_ref), custom_call_target="tpu_custom_call" | custom-call | flops 65536 | bytes 262144 | tf_op jit(solution)/shard_map/pallas_call | solution.py:372
  (1 shorter events, 0.0 us)
Async XLA Ops:
  2.5 6.5 %collective-permute-start = (f32[32,8,256]{2,1,0:T(8,128)S(1)}, f32[32,8,256]{2,1,0:T(8,128)S(1)}, u32[]{:S(2)}, u32[]{:S(2)}) collective-permute-start(f32[32,8,256]{2,1,0:T(8,128)S(1)} %get-tuple-element.23.own_ref), channel_id=1, source_target_pairs={{0,1},{1,0},{2,3},{3,2},{4,5},{5,4},{6,7},{7,6},{8,9},{9,8},{10,11... | collective-permute-start | bytes 786440 | tf_op jit(solution)/shard_map/ppermute | solution.py:413
  2.6 22.1 %copy-start = (bf16[256,384]{1,0:T(8,128)(2,1)S(1)}, bf16[256,384]{1,0:T(8,128)(2,1)}, u32[]{:S(2)}) copy-start(bf16[256,384]{1,0:T(8,128)(2,1)} %constant.8.clone.spread_ref) | copy-start | bytes 589828
  2.6 8.6 %collective-permute-start.1 = (f32[16,256]{1,0:T(8,128)S(1)}, f32[16,256]{1,0:T(8,128)S(1)}, u32[]{:S(2)}, u32[]{:S(2)}) collective-permute-start(f32[16,256]{1,0:T(8,128)S(1)} %get-tuple-element.20.own_ref), channel_id=1, source_target_pairs={{0,24},{4,28},{8,16},{12,20},{16,8},{20,12},{24,0},{28,4},{32,56},... | collective-permute-start | bytes 49160 | tf_op jit(solution)/shard_map/ppermute | solution.py:387
  9.0 15.2 %collective-permute-start.2 = (f32[32,8,256]{2,1,0:T(8,128)S(1)}, f32[32,8,256]{2,1,0:T(8,128)S(1)}, u32[]{:S(2)}, u32[]{:S(2)}) collective-permute-start(f32[32,8,256]{2,1,0:T(8,128)S(1)} %get-tuple-element.23.own_ref), channel_id=1, source_target_pairs={{1,2},{2,1},{5,6},{6,5},{9,10},{10,9},{13,14},{14,13},{17,18},{18,... | collective-permute-start | bytes 786440 | tf_op jit(solution)/shard_map/ppermute | solution.py:415
  32.3 4.9 %collective-permute-start.4 = (f32[4,8,256]{2,1,0:T(8,128)S(1)}, f32[4,8,256]{2,1,0:T(8,128)S(1)}, u32[]{:S(2)}, u32[]{:S(2)}) collective-permute-start(f32[4,8,256]{2,1,0:T(8,128)S(1)} %get-tuple-element.29), channel_id=1, source_target_pairs={{0,8},{4,12},{8,0},{12,4},{16,24},{20,28},{24,16},{28,20},{32,40},... | collective-permute-start | bytes 98312 | tf_op jit(solution)/shard_map/ppermute | solution.py:387
  33.9 5.7 %collective-permute-start.5 = (f32[4,8,256]{2,1,0:T(8,128)S(1)}, f32[4,8,256]{2,1,0:T(8,128)S(1)}, u32[]{:S(2)}, u32[]{:S(2)}) collective-permute-start(f32[4,8,256]{2,1,0:T(8,128)S(1)} %get-tuple-element.30), channel_id=1, source_target_pairs={{0,12},{4,8},{8,4},{12,0},{16,28},{20,24},{24,20},{28,16},{32,44},... | collective-permute-start | bytes 98312 | tf_op jit(solution)/shard_map/ppermute | solution.py:387
  35.8 4.1 %collective-permute-start.3 = (f32[4,8,256]{2,1,0:T(8,128)S(1)}, f32[4,8,256]{2,1,0:T(8,128)S(1)}, u32[]{:S(2)}, u32[]{:S(2)}) collective-permute-start(f32[4,8,256]{2,1,0:T(8,128)S(1)} %get-tuple-element.26), channel_id=1, source_target_pairs={{0,4},{4,0},{8,12},{12,8},{16,20},{20,16},{24,28},{28,24},{32,36},... | collective-permute-start | bytes 98312 | tf_op jit(solution)/shard_map/ppermute | solution.py:387

commit v7 on v6

--- a/solution.py
+++ b/solution.py
@@ -19,7 +19,6 @@
 STRIP = 4
 LANES = 128
 KDIM = TS * 48
-EXACT = lax.Precision.HIGHEST
 VMEM = pl.BlockSpec(memory_space=pltpu.VMEM)
 HBM = pl.BlockSpec(memory_space=pltpu.HBM)
 
@@ -121,7 +120,7 @@
     c, s = np.cos(pair), np.sin(pair)
     ahead = np.block([[c, s], [-s, c]])
     back = np.block([[c, -s], [s, c]])
-    return two_terms(right), np.float32(np.stack([ahead, back]))
+    return two_terms(right), two_terms(np.stack([ahead, back]))
 
 
 def spread_table():
@@ -162,8 +161,14 @@
     def flat(ref):
         return jnp.concatenate([ref[c].astype(jnp.float32) for c in range(TS)], axis=1)
 
-    def exact(a, b):
-        return jnp.dot(a, b, precision=EXACT, preferred_element_type=jnp.float32)
+    def across_rows(i, value):
+        rows = value.shape[0]
+        high, low = halves(value)
+        table = jnp.concatenate([small_ref[0, i], small_ref[1, i]], axis=0)
+        out = jnp.dot(table, high, preferred_element_type=jnp.float32)
+        return out[:rows] + (
+            out[rows:] + jnp.dot(small_ref[0, i], low, preferred_element_type=jnp.float32)
+        )
 
     def product(value, lanes):
         rows = value.shape[0]
@@ -172,13 +177,15 @@
         low = jnp.dot(both[:rows], right_ref[1, :, lanes], preferred_element_type=jnp.float32)
         return out[:rows] + (out[rows:] + low)
 
-    for copy in copies:
+    for copy in copies[:2]:
         copy.wait()
     spec = product(flat(template_ref), slice(0, 2 * width))
     spec = jnp.concatenate([spec[:, :width], spec[:, width:]], axis=0)
+    for copy in copies[2:]:
+        copy.wait()
     keep = flat(wedge_ref)
-    spec = exact(small_ref[0], spec) * jnp.concatenate([keep, keep], axis=0)
-    spec = exact(small_ref[1], spec)
+    spec = across_rows(0, spec) * jnp.concatenate([keep, keep], axis=0)
+    spec = across_rows(1, spec)
     filt = product(spec[:TS], slice(0, width)) + product(spec[TS:], slice(width, 2 * width))
     filt = filt * (1.0 / float(TS**3))
     centered = filt - jnp.sum(filt) * (1.0 / float(TS**3))
@@ -394,7 +401,7 @@
             pltpu.VMEM((TS, TS, TS), f32),
             pltpu.VMEM((TS, TS, TS), jnp.int32),
             pltpu.VMEM(right.shape, bf16),
-            pltpu.VMEM(small.shape, f32),
+            pltpu.VMEM(small.shape, bf16),
             pltpu.VMEM((NY // LANES, SLAB, NF, LANES), f32),
             pltpu.SemaphoreType.DMA((12,)),
         ],

time: 41 us -> 41 us (level)
  no operation moved by 1% of the time
where the time goes in v7:
time: 41 us; the launch traced here: 40.5 us
  blocking collectives  13 us (32%)
  starting transfers between devices  12.2 us (30%)
  Pallas kernels  11.6 us (28%)
  waiting for transfers between devices  3.58 us (9%)
    all_to_all x1, blocking collectives, shards(): lax.all_to_all(fan, 'orient', 0, 0, tiled=True, axis_index_groups=near)  13 us
    pallas_call x6, Pallas kernels, call(): pl.pallas_call(kernel, out_shape=outs, in_specs=specs, out_specs=[VMEM] *...  11.6 us
    ppermute x4, starting transfers between devices, swap(): return lax.ppermute(value, 'orient', [(i, i ^ mask) for i in range(count)])  9.96 us
    ppermute x4, waiting for transfers between devices, swap(): return lax.ppermute(value, 'orient', [(i, i ^ mask) for i in range(count)])  3.57 us
    ppermute x1, starting transfers between devices, shards(): across = lax.ppermute(later, 'zslab', [(1, 2), (2, 1)])  2.16 us
  transfers between devices with their start and end apart: 6, of which 3 were waited for; matrix products, arithmetic and copies ran while one was open for 0% of the time, Pallas kernels for 1%

profile of v7, /device:TPU:4, one launch (start us, length us, event | category | flops | bytes accessed | tf_op | source)
XLA Modules:
  0.0 40.5 jit_solution(13143697245596510954)
XLA Ops:
  0.0 2.4 %shard_map.64 = (f32[16,256]{1,0:T(8,128)S(1)}, f32[32,8,256]{2,1,0:T(8,128)S(1)}) custom-call(f32[16,16,16]{2,1,0:T(8,128)} %bitcast.3, s32[16,16,16]{2,1,0:T(8,128)} %wedge_hbm.1, f32[8,256,256]{2,1,0:T(8,128)} %volume_hbm.1, bf16[2,256,512]{2,1,0:T(8,128)(2,1)} %constant.6.clone.right_hbm, bf16[2,2,32,32]{3,2,1,0:T(8,128)(2,1)} %constant.7.clone.small_hbm), custom_call_target="tpu_custom_call" | custom-call | flops 4194304 | bytes 1048576 | tf_op jit(solution)/shard_map/pallas_call | solution.py:379
  2.4 0.1 collective-permute-start
  2.5 0.0 copy-start
  2.6 6.4 %collective-permute-start.1 = (f32[16,256]{1,0:T(8,128)S(1)}, f32[16,256]{1,0:T(8,128)S(1)}, u32[]{:S(2)}, u32[]{:S(2)}) collective-permute-start(f32[16,256]{1,0:T(8,128)S(1)} %get-tuple-element.20.own_ref), channel_id=1, source_target_pairs={{0,24},{4,28},{8,16},{12,20},{16,8},{20,12},{24,0},{28,4},{32,56},... | collective-permute-start | bytes 49160 | tf_op jit(solution)/shard_map/ppermute | solution.py:394
  8.9 0.0 collective-permute-done.inside_ref
  8.9 2.2 %collective-permute-start.2 = (f32[32,8,256]{2,1,0:T(8,128)S(1)}, f32[32,8,256]{2,1,0:T(8,128)S(1)}, u32[]{:S(2)}, u32[]{:S(2)}) collective-permute-start(f32[32,8,256]{2,1,0:T(8,128)S(1)} %get-tuple-element.23.own_ref), channel_id=1, source_target_pairs={{1,2},{2,1},{5,6},{6,5},{9,10},{10,9},{13,14},{14,13},{17,18},{18,... | collective-permute-start | bytes 786440 | tf_op jit(solution)/shard_map/ppermute | solution.py:422
  11.1 0.0 collective-permute-done.1.other_ref
  11.1 13.0 %all_to_all.5 = f32[8,32,256]{2,1,0:T(8,128)S(1)} all-to-all(f32[8,32,256]{2,1,0:T(8,128)S(1)} %shard_map.65), channel_id=1, replica_groups={{0,32,64,96,128,160,192,224},{4,36,68,100,132,164,196,228},{8,40,72,104..., dimensions={0} | all-to-all | bytes 524288 | tf_op jit(solution)/shard_map/all_to_all | solution.py:415
  24.2 0.0 collective-permute-done.2.across_ref
  24.2 0.4 %shard_map.66 = (bf16[16,128,256]{2,1,0:T(8,128)(2,1)S(1)}, bf16[16,128,256]{2,1,0:T(8,128)(2,1)S(1)}) custom-call(f32[32,8,256]{2,1,0:T(8,128)S(1)} %collective-permute-done.inside_ref, f32[32,8,256]{2,1,0:T(8,128)S(1)} %get-tuple-element.23.own_ref, f32[32,8,256]{2,1,0:T(8,128)S(1)} %collective-permute-done.2.across_ref), custom_call_target="tpu_custom_call" | custom-call | flops 16777216 | bytes 2097152 | tf_op jit(solution)/shard_map/pallas_call | solution.py:379
  24.6 0.0 copy-done
  24.6 7.6 %shard_map.67 = (f32[4,8,256]{2,1,0:T(8,128)S(1)}, f32[4,8,256]{2,1,0:T(8,128)S(1)}, f32[4,8,256]{2,1,0:T(8,128)S(1)}, f32[4,8,256]{2,1,0:T(8,128)S(1)}) custom-call(f32[256,256]{1,0:T(8,128)S(1)} %bitcast.2, bf16[256,384]{1,0:T(8,128)(2,1)S(1)} %copy-done, bf16[16,128,256]{2,1,0:T(8,128)(2,1)S(1)} %get-tuple-element.24.high_ref, ...), custom_call_target="tpu_custom_call" | custom-call | flops 8589934592 | bytes 2097152 | tf_op jit(solution)/shard_map/pallas_call | solution.py:379
  32.2 1.5 %collective-permute-start.4 = (f32[4,8,256]{2,1,0:T(8,128)S(1)}, f32[4,8,256]{2,1,0:T(8,128)S(1)}, u32[]{:S(2)}, u32[]{:S(2)}) collective-permute-start(f32[4,8,256]{2,1,0:T(8,128)S(1)} %get-tuple-element.29), channel_id=1, source_target_pairs={{0,8},{4,12},{8,0},{12,4},{16,24},{20,28},{24,16},{28,20},{32,40},... | collective-permute-start | bytes 98312 | tf_op jit(solution)/shard_map/ppermute | solution.py:394
  33.8 1.9 %collective-permute-start.5 = (f32[4,8,256]{2,1,0:T(8,128)S(1)}, f32[4,8,256]{2,1,0:T(8,128)S(1)}, u32[]{:S(2)}, u32[]{:S(2)}) collective-permute-start(f32[4,8,256]{2,1,0:T(8,128)S(1)} %get-tuple-element.30), channel_id=1, source_target_pairs={{0,12},{4,8},{8,4},{12,0},{16,28},{20,24},{24,20},{28,16},{32,44},... | collective-permute-start | bytes 98312 | tf_op jit(solution)/shard_map/ppermute | solution.py:394
  35.7 0.1 collective-permute-start.3
  35.8 0.5 %shard_map.68.scale_ref = f32[4,8,256]{2,1,0:T(8,128)S(1)} custom-call(f32[32,8,256]{2,1,0:T(8,128)S(1)} %collective-permute-done.inside_ref, f32[32,8,256]{2,1,0:T(8,128)S(1)} %get-tuple-element.23.own_ref, f32[32,8,256]{2,1,0:T(8,128)S(1)} %collective-permute-done.2.across_ref), custom_call_target="tpu_custom_call" | custom-call | flops 4194304 | bytes 1048576 | tf_op jit(solution)/shard_map/pallas_call | solution.py:379
  36.3 0.9 %collective-permute-done.4.c_ref = f32[4,8,256]{2,1,0:T(8,128)S(1)} collective-permute-done((f32[4,8,256]{2,1,0:T(8,128)S(1)}, f32[4,8,256]{2,1,0:T(8,128)S(1)}, u32[]{:S(2)}, u32[]{:S(2)}) %collective-permute-start.4) | collective-permute-done | bytes 32800 | tf_op jit(solution)/shard_map/ppermute | solution.py:394
  37.1 2.4 %collective-permute-done.5.d_ref = f32[4,8,256]{2,1,0:T(8,128)S(1)} collective-permute-done((f32[4,8,256]{2,1,0:T(8,128)S(1)}, f32[4,8,256]{2,1,0:T(8,128)S(1)}, u32[]{:S(2)}, u32[]{:S(2)}) %collective-permute-start.5) | collective-permute-done | bytes 32800 | tf_op jit(solution)/shard_map/ppermute | solution.py:394
  39.5 0.3 collective-permute-done.3.b_ref
  39.9 0.6 %shard_map.69 = f32[8,4,256]{2,1,0:T(4,128)} custom-call(f32[4,8,256]{2,1,0:T(8,128)S(1)} %shard_map.68.scale_ref, f32[4,8,256]{2,1,0:T(8,128)S(1)} %get-tuple-element.28.a_ref, f32[4,8,256]{2,1,0:T(8,128)S(1)} %collective-permute-done.3.b_ref, f32[4,8,256]{2,1,0:T(8,128)S(1)} %collective-permute-done.4.c_ref, f32[4,8,256]{2,1,0:T(8,128)S(1)} %collective-permute-done.5.d_ref), custom_call_target="tpu_custom_call" | custom-call | flops 65536 | bytes 262144 | tf_op jit(solution)/shard_map/pallas_call | solution.py:379
  (1 shorter events, 0.0 us)
Async XLA Ops:
  2.4 6.5 %collective-permute-start = (f32[32,8,256]{2,1,0:T(8,128)S(1)}, f32[32,8,256]{2,1,0:T(8,128)S(1)}, u32[]{:S(2)}, u32[]{:S(2)}) collective-permute-start(f32[32,8,256]{2,1,0:T(8,128)S(1)} %get-tuple-element.23.own_ref), channel_id=1, source_target_pairs={{0,1},{1,0},{2,3},{3,2},{4,5},{5,4},{6,7},{7,6},{8,9},{9,8},{10,11... | collective-permute-start | bytes 786440 | tf_op jit(solution)/shard_map/ppermute | solution.py:420
  2.5 22.1 %copy-start = (bf16[256,384]{1,0:T(8,128)(2,1)S(1)}, bf16[256,384]{1,0:T(8,128)(2,1)}, u32[]{:S(2)}) copy-start(bf16[256,384]{1,0:T(8,128)(2,1)} %constant.8.clone.spread_ref) | copy-start | bytes 589828
  2.6 8.6 %collective-permute-start.1 = (f32[16,256]{1,0:T(8,128)S(1)}, f32[16,256]{1,0:T(8,128)S(1)}, u32[]{:S(2)}, u32[]{:S(2)}) collective-permute-start(f32[16,256]{1,0:T(8,128)S(1)} %get-tuple-element.20.own_ref), channel_id=1, source_target_pairs={{0,24},{4,28},{8,16},{12,20},{16,8},{20,12},{24,0},{28,4},{32,56},... | collective-permute-start | bytes 49160 | tf_op jit(solution)/shard_map/ppermute | solution.py:394
  8.9 15.2 %collective-permute-start.2 = (f32[32,8,256]{2,1,0:T(8,128)S(1)}, f32[32,8,256]{2,1,0:T(8,128)S(1)}, u32[]{:S(2)}, u32[]{:S(2)}) collective-permute-start(f32[32,8,256]{2,1,0:T(8,128)S(1)} %get-tuple-element.23.own_ref), channel_id=1, source_target_pairs={{1,2},{2,1},{5,6},{6,5},{9,10},{10,9},{13,14},{14,13},{17,18},{18,... | collective-permute-start | bytes 786440 | tf_op jit(solution)/shard_map/ppermute | solution.py:422
  32.2 4.9 %collective-permute-start.4 = (f32[4,8,256]{2,1,0:T(8,128)S(1)}, f32[4,8,256]{2,1,0:T(8,128)S(1)}, u32[]{:S(2)}, u32[]{:S(2)}) collective-permute-start(f32[4,8,256]{2,1,0:T(8,128)S(1)} %get-tuple-element.29), channel_id=1, source_target_pairs={{0,8},{4,12},{8,0},{12,4},{16,24},{20,28},{24,16},{28,20},{32,40},... | collective-permute-start | bytes 98312 | tf_op jit(solution)/shard_map/ppermute | solution.py:394
  33.8 5.7 %collective-permute-start.5 = (f32[4,8,256]{2,1,0:T(8,128)S(1)}, f32[4,8,256]{2,1,0:T(8,128)S(1)}, u32[]{:S(2)}, u32[]{:S(2)}) collective-permute-start(f32[4,8,256]{2,1,0:T(8,128)S(1)} %get-tuple-element.30), channel_id=1, source_target_pairs={{0,12},{4,8},{8,4},{12,0},{16,28},{20,24},{24,20},{28,16},{32,44},... | collective-permute-start | bytes 98312 | tf_op jit(solution)/shard_map/ppermute | solution.py:394
  35.7 4.1 %collective-permute-start.3 = (f32[4,8,256]{2,1,0:T(8,128)S(1)}, f32[4,8,256]{2,1,0:T(8,128)S(1)}, u32[]{:S(2)}, u32[]{:S(2)}) collective-permute-start(f32[4,8,256]{2,1,0:T(8,128)S(1)} %get-tuple-element.26), channel_id=1, source_target_pairs={{0,4},{4,0},{8,12},{12,8},{16,20},{20,16},{24,28},{28,24},{32,36},... | collective-permute-start | bytes 98312 | tf_op jit(solution)/shard_map/ppermute | solution.py:394
